TPU v7x, 32 devices: a whole 2x2x4 slice. The times are simulated.
32 devices in a mesh: gx: 16 (over z, x, core), gz: 2 (over y).
Axes of the slice: x: 2, y: 2, z: 4, core: 2. Of those that a mesh axis runs over, the one named last changes fastest.
Arguments:
- u_vel: bfloat16 [512, 384, 768], P('gx', 'gz'), may hold values from -6 to 6
- v_vel: bfloat16 [512, 384, 768], P('gx', 'gz'), may hold values from -6 to 6
- w_vel: bfloat16 [512, 384, 768], P('gx', 'gz'), may hold values from -6 to 6
Outputs:
- pressure: float32 [512, 384, 768], P('gx', 'gz')
- u_new: float32 [512, 384, 768], P('gx', 'gz')
- v_new: float32 [512, 384, 768], P('gx', 'gz')
- w_new: float32 [512, 384, 768], P('gx', 'gz')
All inputs are finite; a program needn't handle non-finite values.
Results may differ from a plain program's by a relative error of at most 0.002.
Values may be sent and summed in bfloat16 or wider, within the bound.
No kernel may reach another device: no remote copies, remote signals or barrier semaphores. Data moves between devices by JAX's collectives and lax.ppermute only.
A program may use at most 192 MiB of HBM per device.

v0:
```python
import math

import jax
import jax.numpy as jnp
from jax import lax
from jax.sharding import PartitionSpec as P


def with_halo(block, sides, width):
    for axis, dim in sides:
        count = lax.axis_size(axis)
        forward = [(i, i + 1) for i in range(count - 1)]
        forward.append((count - 1, 0))
        backward = [(target, source) for source, target in forward]
        low = lax.ppermute(
            lax.slice_in_dim(block, block.shape[dim] - width, None, axis=dim), axis, forward
        )
        high = lax.ppermute(lax.slice_in_dim(block, 0, width, axis=dim), axis, backward)
        block = jnp.concatenate([low, block, high], axis=dim)
    return block


def hartley_table(count):
    index = jnp.arange(count, dtype=jnp.int32)
    product = index[:, None] * index[None, :] % count
    angle = product.astype(jnp.float32) * (2.0 * math.pi / count)
    return jnp.cos(angle) + jnp.sin(angle)


def sine_table(count):
    index = jnp.arange(1, count + 1, dtype=jnp.int32)
    product = index[:, None] * index[None, :] % (2 * (count + 1))
    angle = product.astype(jnp.float32) * (math.pi / (count + 1))
    return math.sqrt(2.0 / (count + 1)) * jnp.sin(angle)


def periodic_eigen(index, count):
    return -4.0 * jnp.sin(index.astype(jnp.float32) * (math.pi / count)) ** 2


def wall_eigen(index, count):
    return -4.0 * jnp.sin((index + 1).astype(jnp.float32) * (math.pi / (2 * count + 2))) ** 2


def wall_slope(field):
    padded = jnp.pad(field, ((0, 0), (0, 0), (1, 1)))
    return 0.5 * (padded[:, :, 2:] - padded[:, :, :-2])


def on_device(u_vel, v_vel, w_vel):
    hi = lax.Precision.HIGHEST
    cx, cz, ny = u_vel.shape
    ngx = lax.axis_size("gx")
    ngz = lax.axis_size("gz")
    nx = cx * ngx
    nz = cz * ngz
    pos_x = lax.axis_index("gx")
    pos_z = lax.axis_index("gz")
    u_wide = with_halo(u_vel, (("gx", 0),), 1)
    w_wide = with_halo(w_vel, (("gz", 1),), 1)
    uf = u_vel.astype(jnp.float32)
    vf = v_vel.astype(jnp.float32)
    wf = w_vel.astype(jnp.float32)
    div = 0.5 * (u_wide[2:].astype(jnp.float32) - u_wide[:-2].astype(jnp.float32))
    div = div + 0.5 * (w_wide[:, 2:].astype(jnp.float32) - w_wide[:, :-2].astype(jnp.float32))
    div = div + wall_slope(vf)
    sine = sine_table(ny)
    hx = hartley_table(nx)
    hz = hartley_table(nz)
    scale = float(nx * nz)
    rows = div.reshape(cx, cz * ny)
    lines = lax.all_to_all(rows, "gx", split_axis=1, concat_axis=0, tiled=True)
    spec_x = jnp.dot(hx, lines, precision=hi)
    planes = lax.all_to_all(spec_x, "gx", split_axis=0, concat_axis=1, tiled=True).reshape(
        cx, cz, ny
    )
    pencil = lax.all_to_all(planes, "gz", split_axis=0, concat_axis=1, tiled=True)
    sub = cx // ngz
    zspec = jnp.einsum("xzy,zk->xky", pencil, hz, precision=hi)
    full = jnp.einsum("xky,ym->xkm", zspec, sine, precision=hi)
    kx_index = pos_x * cx + pos_z * sub + jnp.arange(sub, dtype=jnp.int32)
    kz_index = jnp.arange(nz, dtype=jnp.int32)
    mode_index = jnp.arange(ny, dtype=jnp.int32)
    lam = (
        periodic_eigen(kx_index, nx)[:, None, None]
        + periodic_eigen(kz_index, nz)[None, :, None]
        + wall_eigen(mode_index, ny)[None, None, :]
    )
    solved = full / (lam * scale)
    ymode = jnp.einsum("xkm,my->xky", solved, sine, precision=hi)
    zback = jnp.einsum("xky,zk->xzy", ymode, hz, precision=hi)
    cube = lax.all_to_all(zback, "gz", split_axis=1, concat_axis=0, tiled=True)
    spec_back = lax.all_to_all(
        cube.reshape(cx, cz * ny), "gx", split_axis=1, concat_axis=0, tiled=True
    )
    physical = jnp.dot(hx, spec_back, precision=hi)
    stacked = physical[None]
    home = lax.all_to_all(stacked, "gx", split_axis=1, concat_axis=2, tiled=True)
    layers = home.shape[0]
    fields = home.reshape(layers, cx, cz, ny)
    pressure = fields[0]
    padded = with_halo(pressure, (("gx", 0), ("gz", 1)), 1)
    slope_x = 0.5 * (padded[2:, 1:-1] - padded[:-2, 1:-1])
    slope_z = 0.5 * (padded[1:-1, 2:] - padded[1:-1, :-2])
    u_new = uf - slope_x
    v_new = vf - wall_slope(pressure)
    w_new = wf - slope_z
    return (pressure, u_new, v_new, w_new)


def solution(mesh):
    return jax.shard_map(
        on_device,
        mesh=mesh,
        in_specs=(P("gx", "gz", None), P("gx", "gz", None), P("gx", "gz", None)),
        out_specs=(
            P("gx", "gz", None),
            P("gx", "gz", None),
            P("gx", "gz", None),
            P("gx", "gz", None),
        ),
        check_vma=False,
    )
```

profile of v0, /device:TPU:1, one launch (start us, length us, event | category | flops | bytes accessed | tf_op | source)
XLA Modules:
  0.0 2752.8 jit_solution(2103367460620175343)
XLA Ops:
  7.3 12.9 convert_element_type.81
  20.2 37.6 %fusion.2 = f32[32,192,768]{2,1,0:T(8,128)} fusion(f32[32,192,768]{2,1,0:T(8,128)} %convert_element_type.81, bf16[32,192,768]{2,1,0:T(8,128)(2,1)} %param.5, bf16[32,1,768]{2,1,0:T(2,128)(2,1)S(1)} %collective-permute-done.3, bf16[32,1,768]{2,1,0:T(2,128)(2,1)S(1)} %collective-permute-done.2, bf16[32,192,768]{2,1,0:T(8,128)(2,1)} %param.3, ...), kind=kLoop, calls=%fused_computation.6 | loop fusion | flops 103809024 | bytes 57311232 | tf_op jit(solution)/shard_map/add | solution.py:66
  57.8 20.5 all_to_all.73
  78.3 19.6 copy.50
  97.9 8.9 all-to-all-start
  112.4 327.9 %all-to-all-done = f32[32,16,9216]{2,0,1:T(8,128)} async-done(((f32[32,16,9216]{2,0,1:T(8,128)}), f32[32,16,9216]{2,0,1:T(8,128)}, u32[]{:S(2)}, u32[]{:S(2)}) %all-to-all-start) | async-done | bytes 18874400 | tf_op jit(solution)/shard_map/all_to_all | solution.py:72
  440.3 33.5 %fusion.49 = f32[16,32,9216]{2,1,0:T(8,128)S(1)} fusion(f32[512,9216,1]{1,0,2:T(8,128)} %bitcast.5, f32[16,32,512]{2,1,0:T(8,128)} %fusion.147), kind=kOutput, calls=%fused_computation.71 | convolution fusion | flops 28991029248 | bytes 38797312 | tf_op jit(solution)/shard_map/dot_general | solution.py:73
  473.8 485.3 %all_to_all.99 = f32[16,32,9216]{2,1,0:T(8,128)S(1)} all-to-all(f32[16,32,9216]{2,1,0:T(8,128)S(1)} %fusion.49), channel_id=1, replica_groups=mesh['gx'=16,'gz'=2] {'gx'}, dimensions={0} | all-to-all | bytes 37748736 | tf_op jit(solution)/shard_map/all_to_all | solution.py:74
  959.1 18.8 copy.51
  977.8 20.4 reshape.170
  998.3 10.9 all-to-all-start.2
  1011.8 9.2 fusion.141
  1021.0 193.2 %all-to-all-done.2 = f32[32,192,768]{2,1,0:T(8,128)} async-done(((f32[32,192,768]{2,1,0:T(8,128)}), f32[32,192,768]{2,1,0:T(8,128)}, u32[]{:S(2)}, u32[]{:S(2)}) %all-to-all-start.2) | async-done | bytes 18874400 | tf_op jit(solution)/shard_map/all_to_all | solution.py:77
  1214.2 7.4 copy.52
  1221.5 33.5 %fusion.71 = f32[384,16,768]{2,0,1:T(8,128)} fusion(f32[16,384,768]{2,1,0:T(8,128)S(1)} %bitcast.75, f32[384,384,1]{1,0,2:T(8,128)S(1)} %fusion.149), kind=kOutput, calls=%fused_computation.88 | convolution fusion | flops 21743271936 | bytes 38338560 | tf_op jit(solution)/shard_map/xzy,zk->xky/dot_general | solution.py:79
  1255.0 52.9 %fusion.12 = f32[16,384,768]{2,1,0:T(8,128)S(1)} fusion(f32[384,16,768]{2,0,1:T(8,128)} %fusion.71, f32[768,768,1]{1,0,2:T(8,128)S(1)} %fusion.141), kind=kOutput, calls=%fused_computation.20 | convolution fusion | flops 43486543872 | bytes 40108032 | tf_op jit(solution)/shard_map/xky,ym->xkm/dot_general | solution.py:80
  1315.2 71.3 %fusion.14 = f32[16,384,768]{2,1,0:T(8,128)} fusion(s32[768]{0:T(1024)S(1)} %iota_add_fusion, f32[16,384,768]{2,1,0:T(8,128)} %fusion.143), kind=kOutput, calls=%fused_computation.24 | convolution fusion | flops 43492442112 | bytes 37751808 | tf_op jit(solution)/shard_map/xkm,my->xky/dot_general | solution.py:90
  1386.5 53.2 %convolution_bitcast_fusion.1 = f32[16,384,768]{2,1,0:T(8,128)S(1)} fusion(f32[16,384,768]{2,1,0:T(8,128)} %fusion.14), kind=kOutput, calls=%fused_computation.36 | convolution fusion | flops 21744746496 | bytes 37748736 | tf_op jit(solution)/shard_map/xky,zk->xzy/dot_general | solution.py:91
  1439.7 22.8 copy.54
  1462.6 210.3 %all_to_all.100 = f32[16,384,768]{2,0,1:T(8,128)S(1)} all-to-all(f32[16,384,768]{2,0,1:T(8,128)} %copy.54), channel_id=1, replica_groups=mesh['gx'=16,'gz'=2] {'gz'}, dimensions={1} | all-to-all | bytes 37748736 | tf_op jit(solution)/shard_map/all_to_all | solution.py:92
  1672.8 21.5 copy.68
  1694.3 20.5 all_to_all.86
  1714.8 19.6 copy.56
  1734.5 7.4 all-to-all-start.4
  1746.0 329.4 %all-to-all-done.4 = f32[32,16,9216]{2,0,1:T(8,128)} async-done(((f32[32,16,9216]{2,0,1:T(8,128)}), f32[32,16,9216]{2,0,1:T(8,128)}, u32[]{:S(2)}, u32[]{:S(2)}) %all-to-all-start.4) | async-done | bytes 18874400 | tf_op jit(solution)/shard_map/all_to_all | solution.py:93
  2075.5 35.2 %convolution_bitcast_fusion = f32[1,512,9216]{2,1,0:T(8,128)} fusion(f32[512,9216]{1,0:T(8,128)} %bitcast.16, f32[512,512]{1,0:T(8,128)S(1)} %fusion.145), kind=kOutput, calls=%fused_computation.28 | convolution fusion | flops 28991029248 | bytes 38797312 | tf_op jit(solution)/shard_map/dot_general | solution.py:96
  2110.7 21.6 copy.57
  2132.3 485.4 %all_to_all.101 = f32[1,512,9216]{2,0,1:T(1,128)} all-to-all(f32[1,512,9216]{2,0,1:T(1,128)S(1)} %copy.57), channel_id=1, replica_groups=mesh['gx'=16,'gz'=2] {'gx'}, dimensions={1} | all-to-all | bytes 37748736 | tf_op jit(solution)/shard_map/all_to_all | solution.py:98
  2617.6 17.0 copy.67
  2642.6 20.4 squeeze_reshape.3
  2663.9 55.6 %constant_dynamic-update-slice_fusion.1 = (f32[34,192,768]{2,1,0:T(8,128)}, f32[32,192,768]{2,1,0:T(8,128)}, f32[32,192,768]{2,1,0:T(8,128)}) fusion(f32[34,192,768]{2,1,0:T(8,128)} %constant_dynamic-update-slice_fusion.2, f32[32,192,768]{2,1,0:T(8,128)} %squeeze_reshape.3, bf16[32,192,768]{2,1,0:T(8,128)(2,1)} %param.4, ...), kind=kLoop, calls=%fused_computation.113 | loop fusion | flops 47185920 | bytes 95551488
  2727.2 25.3 fusion.8
  (40 shorter events, 42.8 us)
Async XLA Ops:
  1.7 18.4 collective-permute-start
  1.8 18.3 collective-permute-start.1
  5.7 14.4 collective-permute-start.2
  7.0 13.1 collective-permute-start.3
  97.9 342.4 %all-to-all-start = ((f32[32,16,9216]{2,0,1:T(8,128)}), f32[32,16,9216]{2,0,1:T(8,128)}, u32[]{:S(2)}, u32[]{:S(2)}) async-start(f32[32,16,9216]{2,0,1:T(8,128)} %copy.50), calls=%async_computation | async-start | bytes 37748736 | tf_op jit(solution)/shard_map/all_to_all | solution.py:72
  998.3 215.9 %all-to-all-start.2 = ((f32[32,192,768]{2,1,0:T(8,128)}), f32[32,192,768]{2,1,0:T(8,128)}, u32[]{:S(2)}, u32[]{:S(2)}) async-start(f32[32,192,768]{2,1,0:T(8,128)} %reshape.170), calls=%async_computation.2 | async-start | bytes 37748736 | tf_op jit(solution)/shard_map/all_to_all | solution.py:77
  1734.5 341.0 %all-to-all-start.4 = ((f32[32,16,9216]{2,0,1:T(8,128)}), f32[32,16,9216]{2,0,1:T(8,128)}, u32[]{:S(2)}, u32[]{:S(2)}) async-start(f32[32,16,9216]{2,0,1:T(8,128)} %copy.56), calls=%async_computation.4 | async-start | bytes 37748736 | tf_op jit(solution)/shard_map/all_to_all | solution.py:93
  2634.6 6.9 copy-start
  2641.7 21.3 collective-permute-start.5
  2642.6 21.4 collective-permute-start.4
  2722.0 3.8 collective-permute-start.7
  2722.1 5.0 collective-permute-start.6
where the time goes:
time: 2770 us; the launch traced here: 2750 us
  blocking collectives  1180 us (43%)
  waiting for transfers between devices  854 us (31%)
  matrix products  280 us (10%)
  local copies, waits for them, and re-layouts  243 us (9%)
  other arithmetic  160 us (6%)
  starting transfers between devices  33.8 us (1%)
    all_to_all x1, blocking collectives, on_device(): lax.all_to_all(stacked, 'gx', split_axis=1, concat_axis=2, tiled=True)  485 us
    all_to_all x1, blocking collectives, on_device(): lax.all_to_all(spec_x, 'gx', split_axis=0, concat_axis=1, tiled=True)  485 us
    all_to_all x1, waiting for transfers between devices, on_device(): lax.all_to_all(cube.reshape(cx, cz * ny), 'gx', split_axis=1, concat_axis...  329 us
    all_to_all x1, waiting for transfers between devices, on_device(): lines = lax.all_to_all(rows, 'gx', split_axis=1, concat_axis=0, tiled=True)  328 us
    all_to_all x1, blocking collectives, on_device(): cube = lax.all_to_all(zback, 'gz', split_axis=1, concat_axis=0, tiled=True)  210 us
    all_to_all x1, waiting for transfers between devices, on_device(): lax.all_to_all(planes, 'gz', split_axis=0, concat_axis=1, tiled=True)  193 us
    dot_general x1, matrix products, on_device(): ymode = jnp.einsum('xkm,my->xky', solved, sine, precision=hi)  71.3 us
    unnamed x1, other arithmetic  55.6 us
  transfers between devices with their start and end apart: 11, of which 5 were waited for; matrix products, arithmetic and copies ran while one was open for 2% of the time, Pallas kernels for 0%

commit v1 on v0

v1 whole, which is shorter than its diff:
```python
import functools
import math
import ml_dtypes
import numpy as np
import jax
import jax.numpy as jnp
from jax import lax
from jax.experimental import pallas as pl
from jax.experimental.pallas import tpu as pltpu
from jax.sharding import PartitionSpec as P

HI = lax.Precision.HIGHEST


def slab_order(count):
    return np.concatenate([np.arange(0, count, 2), np.arange(1, count, 2)])


def slab_table(count):
    order = slab_order(count)
    cell = np.arange(count)
    table = math.sqrt(2.0 / count) * np.sin(np.pi * np.outer(order, cell) / count)
    table[0, 0] = 1.0
    return table


def sine_table(count):
    index = np.arange(1, count + 1)
    angle = np.outer(index, index) % (2 * (count + 1)) * (np.pi / (count + 1))
    return math.sqrt(2.0 / (count + 1)) * np.sin(angle)


def hartley_table(count):
    index = np.arange(count)
    angle = np.outer(index, index) % count * (2.0 * np.pi / count)
    return np.cos(angle) + np.sin(angle)


def wall_part(count):
    return np.sin(np.arange(1, count + 1) * (np.pi / (2 * count + 2))) ** 2


def shift_pair(block, axis, dim):
    count = lax.axis_size(axis)
    forward = [(i, (i + 1) % count) for i in range(count)]
    backward = [(target, source) for source, target in forward]
    low = lax.ppermute(lax.slice_in_dim(block, block.shape[dim] - 1, None, axis=dim), axis, forward)
    high = lax.ppermute(lax.slice_in_dim(block, 0, 1, axis=dim), axis, backward)
    return low, high


def owner(recv, ngx, ngz, n, m_cells, ny):
    nx, half = ngx * n, m_cells // 2
    mc = recv.shape[1]
    got = recv.reshape(ngx, ngz, mc, -1)
    a_end, b_end = got[..., :m_cells], got[..., m_cells:2 * m_cells]
    t_e, t_o, f_int = (got[..., 2 * m_cells + i * n:2 * m_cells + (i + 1) * n] for i in range(3))
    first = (lax.axis_index("gx") * ngz + lax.axis_index("gz")) * mc
    order = slab_order(m_cells)
    wall = lax.dynamic_slice_in_dim(jnp.asarray(wall_part(ny), jnp.float32), first, mc)
    across = jnp.asarray(np.sin(np.pi * order / (2 * m_cells)) ** 2, jnp.float32)
    s = jnp.sqrt(wall[:, None] + across)
    theta = 2.0 * jnp.log1p(s + s * s / (1.0 + jnp.sqrt(1.0 + s * s)))
    real = jnp.asarray(order > 0, jnp.float32)
    power = lambda e: jnp.exp(-theta * e)
    edge = jnp.asarray(slab_table(m_cells)[:, 1] * (order > 0), jnp.float32)
    steps = jnp.arange(n, dtype=jnp.float32)[None, :, None]
    rise = edge * jnp.exp(-theta[:, None, :] * (steps + 1.0))
    fall = edge * jnp.exp(-theta[:, None, :] * (n - 1.0 - steps))
    r_n = power(float(n)) * real
    wrap = 1.0 / (1.0 - power(float(nx)) * real)
    gain = real * power(1.0) / (1.0 - power(2.0))

    def carries(ends, back):
        seq = list(range(ngx))[::-1] if back else list(range(ngx))
        total = ends[seq[0]]
        for d in seq[1:]:
            total = r_n * total + ends[d]
        now = total * wrap
        out = [None] * ngx
        for d in seq:
            out[d] = now
            now = r_n * now + ends[d]
        return jnp.stack(out)

    def both(fn):
        return [fn(slice(0, half)), fn(slice(half, None))]

    a_in, b_in = carries(a_end, False), carries(b_end, True)
    add_e, add_o = both(lambda q: jnp.einsum("djmq,mxq->djmx", a_in[..., q] * gain[:, q], rise[..., q], precision=HI)
                        + jnp.einsum("djmq,mxq->djmx", b_in[..., q] * gain[:, q], fall[..., q], precision=HI))
    t_e, t_o = t_e - add_e, t_o - add_o
    rhs = f_int - (t_o + t_e) - jnp.roll(t_o - t_e, 1, 1)
    hx = jnp.asarray(hartley_table(nx), jnp.float32)
    hj = jnp.asarray(hartley_table(ngz), jnp.float32)
    line = jnp.einsum("djmx,ij->imdx", rhs, hj, precision=HI).reshape(ngz * mc, nx)
    spec = jnp.dot(line, hx, precision=HI).reshape(ngz, mc, nx)
    s2 = wall[:, None] + jnp.asarray(np.sin(np.pi * np.arange(nx) / nx) ** 2, jnp.float32)
    sq = jnp.sqrt(s2)
    root = jnp.sqrt(1.0 + s2)
    decay = jnp.exp(-2.0 * m_cells * jnp.log1p(sq + s2 / (1.0 + root)))
    cosj = jnp.asarray(np.cos(2 * np.pi * np.arange(ngz) / ngz), jnp.float32)[:, None, None]
    schur = -4.0 * sq * root * (1.0 + decay * decay - 2.0 * decay * cosj) / (1.0 - decay * decay)
    spec = spec / (schur * float(nx * ngz))
    line = jnp.dot(spec.reshape(ngz * mc, nx), hx, precision=HI).reshape(ngz, mc, nx)
    g = jnp.einsum("imx,ij->jmx", line, hj, precision=HI)
    g_next = jnp.roll(g, -1, 0)
    blocks = lambda f: jnp.moveaxis(f.reshape(ngz, mc, ngx, n), 2, 0)
    even, odd = blocks(g - g_next), blocks(g + g_next)
    pick = lambda t: jnp.concatenate([jnp.einsum("djmx,mxq->djmq", even, t[..., :half], precision=HI),
                                      jnp.einsum("djmx,mxq->djmq", odd, t[..., half:], precision=HI)], -1)
    a_in = carries(a_end - pick(fall), False)
    b_in = carries(b_end - pick(rise), True)

    def windows(f):
        wide = jnp.concatenate([f[..., -2:], f, f[..., :6]], -1)
        return jnp.stack([wide[..., d * n:d * n + n + 8] for d in range(ngx)])

    out = jnp.concatenate([a_in, b_in, windows(g), windows(g_next)], -1)
    return out.reshape(ngx * ngz, mc, -1)


VMEM_LIMIT = 60 * 1024 * 1024
EXTRA = 16


def split_np(table):
    wide = np.asarray(table, np.float32)
    high = wide.astype(ml_dtypes.bfloat16)
    low = (np.asarray(table, np.float64) - high.astype(np.float64)).astype(ml_dtypes.bfloat16)
    return jnp.asarray(high), jnp.asarray(low)


def split(value):
    high = value.astype(jnp.bfloat16)
    return high, (value - high.astype(jnp.float32)).astype(jnp.bfloat16)


def dot(a, b):
    return jnp.dot(a, b, preferred_element_type=jnp.float32)


def dot3(a, b):
    return dot(a[0], b[0]) + (dot(a[1], b[0]) + dot(a[0], b[1]))


def mode_planes(m_cells, ny):
    order = slab_order(m_cells)
    s = np.sqrt(np.sin(np.pi * order / (2 * m_cells))[:, None] ** 2 + wall_part(ny)[None])
    r = (np.sqrt(1 + s * s) - s) ** 2 * (order > 0)[:, None]
    edge = slab_table(m_cells)[:, 1] * (order > 0)
    edge = np.broadcast_to(edge[:, None], r.shape)
    return jnp.asarray(r, jnp.float32), jnp.asarray(edge, jnp.float32)


def chunks(rows, size=24):
    half = rows // 2
    size = math.gcd(size, half)
    return [slice(i, i + size) for i in range(0, rows, size)]


def wall_gap(field):
    ny = field.shape[1]
    at = lax.broadcasted_iota(jnp.int32, field.shape, 1)
    after = jnp.where(at == ny - 1, 0.0, pltpu.roll(field, ny - 1, 1))
    before = jnp.where(at == 0, 0.0, pltpu.roll(field, 1, 1))
    return after - before


def front_kernel(planes, steps, u_lo, u_hi, u_prev, u, u_next, v, w, w_lo, w_hi, sh, sl, th, tl, r, edge,
                 a_out, pay, a_all, now, xh, xl, hits):
    i = pl.program_id(0)
    mz, ny = now.shape
    n = planes * steps
    half = mz // 2
    f = lambda t: t.astype(jnp.float32)

    @pl.when(i == 0)
    def _():
        now[...] = jnp.zeros_like(now)

    row = lax.broadcasted_iota(jnp.int32, (mz, ny), 0)
    for p in range(planes):
        if p == 0:
            before = jnp.where(i == 0, f(u_lo[0]), f(u_prev[0]))
        else:
            before = f(u[p - 1])
        if p == planes - 1:
            after = jnp.where(i == steps - 1, f(u_hi[0]), f(u_next[0]))
        else:
            after = f(u[p + 1])
        mid = f(w[p])
        w_after = jnp.where(row == mz - 1, w_hi[p], pltpu.roll(mid, mz - 1, 0))
        w_before = jnp.where(row == 0, w_lo[p], pltpu.roll(mid, 1, 0))
        div = 0.5 * ((after - before) + (w_after - w_before) + wall_gap(f(v[p])))
        high, low = split(div)
        xh[p * mz:(p + 1) * mz, :] = high
        xl[p * mz:(p + 1) * mz, :] = low
    spec = dot3((xh[...], xl[...]), (sh[...], sl[...]))
    for p in range(planes):
        part = split(spec[p * mz:(p + 1) * mz])
        a = r[...] * now[...] + dot3((th[...], tl[...]), part)
        now[...] = a
        a_out[p] = a
        a_all[i * planes + p] = a

    @pl.when(i == steps - 1)
    def _():
        pay[0:mz, :] = now[...]
        hits[...] = jnp.zeros_like(hits)
        for rows in chunks(mz, 8):
            rr = r[rows, :]
            ee = edge[rows, :]
            side = 0 if rows.start < half else 1
            start = -(rr * rr / (1.0 - rr * rr)) * now[rows, :]

            def body(k, part):
                x = n - 1 - k
                part = rr * (part - a_all[x, rows, :])
                hits[side, x] = hits[side, x] + ee * part
                return part

            part = lax.fori_loop(0, n, body, start)
            pay[mz + rows.start:mz + rows.stop, :] = -(1.0 - rr * rr) * part
        pay[2 * mz:2 * mz + n, :] = jnp.sum(hits[0], axis=1)
        pay[2 * mz + n:2 * mz + 2 * n, :] = jnp.sum(hits[1], axis=1)
        for x in range(n):
            pay[2 * mz + 2 * n + x:2 * mz + 2 * n + x + 1, :] = a_all[x, 0:1, :]


def front(u, v, w, u_lo, u_hi, w_lo, w_hi):
    n, mz, ny = u.shape
    planes = 4
    steps = n // planes
    r, edge = mode_planes(mz, ny)
    whole = lambda a: pl.BlockSpec(a.shape, lambda i: (0,) * a.ndim, pipeline_mode=pl.Buffered(1))
    group = pl.BlockSpec((planes, mz, ny), lambda i: (i, 0, 0))
    lines = pl.BlockSpec((planes, 1, ny), lambda i: (i, 0, 0))
    tables = split_np(sine_table(ny)) + split_np(slab_table(mz)) + (r, edge)
    w_lo, w_hi = w_lo.astype(jnp.float32), w_hi.astype(jnp.float32)
    prev = pl.BlockSpec((1, mz, ny), lambda i: (jnp.maximum(i * planes - 1, 0), 0, 0))
    after = pl.BlockSpec((1, mz, ny), lambda i: (jnp.minimum(i * planes + planes, n - 1), 0, 0))
    rows = 2 * mz + 3 * n
    return pl.pallas_call(
        functools.partial(front_kernel, planes, steps),
        grid=(steps,),
        in_specs=[whole(u_lo), whole(u_hi), prev, group, after, group, group, lines, lines] + [whole(t) for t in tables],
        out_specs=[group, pl.BlockSpec((rows, ny), lambda i: (0, 0), pipeline_mode=pl.Buffered(1))],
        out_shape=[jax.ShapeDtypeStruct((n, mz, ny), jnp.float32), jax.ShapeDtypeStruct((rows, ny), jnp.float32)],
        scratch_shapes=[pltpu.VMEM((n, mz, ny), jnp.float32), pltpu.VMEM((mz, ny), jnp.float32),
                        pltpu.VMEM((planes * mz, ny), jnp.bfloat16), pltpu.VMEM((planes * mz, ny), jnp.bfloat16),
                        pltpu.VMEM((2, n, 8, ny), jnp.float32)],
        compiler_params=pltpu.CompilerParams(dimension_semantics=("arbitrary",), vmem_limit_bytes=VMEM_LIMIT),
        name="front",
    )(u_lo, u_hi, u, u, u, v, w, w_lo, w_hi, *tables)


def back_kernel(n, a_hbm, a_in, b_in, g, g_next, u, v, w, sh, sl, th, tl, r, edge, stiff,
                p_out, u_out, v_out, w_out, a_all, now, xh, xl, pbuf, sems):
    s = pl.program_id(0)
    mz, ny = now.shape
    half = mz // 2
    tall = mz + EXTRA

    @pl.when(s == 0)
    def _():
        copies = [pltpu.make_async_copy(a_hbm.at[x], a_all.at[x + 1], sems.at[x]) for x in range(n)]
        for copy in copies:
            copy.start()
        now[...] = a_in[...]
        a_all[0] = a_in[...]

        def body(x, carry):
            pltpu.make_async_copy(a_hbm.at[x], a_all.at[x + 1], sems.at[x]).wait()
            here, there = g[pl.ds(x + 2, 1), :], g_next[pl.ds(x + 2, 1), :]
            for rows in chunks(mz):
                mix = here - there if rows.start < half else here + there
                new = r[rows, :] * now[rows, :] - edge[rows, :] * mix
                now[rows, :] = new
                a_all[x + 1, rows, :] = a_all[x + 1, rows, :] + new
            return carry

        lax.fori_loop(0, n, body, 0)
        for rows in chunks(mz):
            rr = r[rows, :]
            now[rows, :] = -(rr * rr * a_all[n, rows, :] + b_in[rows, :]) / (1.0 - rr * rr)

    for t in range(2):
        x = n - 2 * s - t

        def advance():
            now[...] = r[...] * (now[...] - a_all[x + 1])

        if t == 0:
            pl.when(s > 0)(advance)
        else:
            advance()
        now[0:1, :] = g[pl.ds(x + 2, 1), :]
        pz = dot3((th[...], tl[...]), split(now[...]))
        now[0:1, :] = jnp.zeros((1, ny), jnp.float32)
        high, low = split(pz)
        base = t * tall
        xh[base:base + mz, :] = high
        xl[base:base + mz, :] = low
        under = (a_all[jnp.minimum(x + 1, n), 0:1, :] - pz[1:2, :] - g[pl.ds(x + 3, 1), :] - g[pl.ds(x + 1, 1), :]
                 + stiff[...] * g[pl.ds(x + 2, 1), :])
        at = lax.broadcasted_iota(jnp.int32, (EXTRA, ny), 0)
        extra = jnp.where(at == 0, g_next[pl.ds(x + 2, 1), :], jnp.where(at == EXTRA - 1, under, 0.0))
        high, low = split(extra)
        xh[base + mz:base + tall, :] = high
        xl[base + mz:base + tall, :] = low
    slot = lax.rem(s, 2)
    fresh = dot3((xh[...], xl[...]), (sh[...], sl[...]))
    for t in range(2):
        pbuf[slot, t] = fresh[t * tall:(t + 1) * tall]

    @pl.when(s > 0)
    def _():
        f = lambda a: a.astype(jnp.float32)
        trio = ((1, pbuf[1 - slot, 0, :mz], pbuf[1 - slot, 1], pbuf[slot, 0, :mz]),
                (0, pbuf[1 - slot, 1, :mz], pbuf[slot, 0], pbuf[slot, 1, :mz]))
        for k, after, full, before in trio:
            mid = full[:mz]
            p_out[k] = mid
            u_out[k] = f(u[k]) - 0.5 * (after - before)
            v_out[k] = f(v[k]) - 0.5 * wall_gap(mid)
            up, down = pltpu.roll(full, tall - 1, 0)[:mz], pltpu.roll(full, 1, 0)[:mz]
            w_out[k] = f(w[k]) - 0.5 * (up - down)


def back(a_loc, ret, u, v, w):
    n, mz, ny = u.shape
    ret = ret.T
    a_in, b_in = ret[:mz], ret[mz:2 * mz]
    g, g_next = ret[2 * mz:2 * mz + n + 8], ret[2 * mz + n + 8:]
    r, edge = mode_planes(mz, ny)
    stiff = jnp.asarray(4.0 + 4.0 * wall_part(ny)[None], jnp.float32)
    tables = split_np(sine_table(ny)) + split_np(slab_table(mz).T) + (r, edge, stiff)
    whole = lambda a: pl.BlockSpec(a.shape, lambda i: (0,) * a.ndim, pipeline_mode=pl.Buffered(1))
    pair = pl.BlockSpec((2, mz, ny), lambda s: (jnp.minimum(n // 2 - s, n // 2 - 1), 0, 0))
    shape = jax.ShapeDtypeStruct((n, mz, ny), jnp.float32)
    tall = mz + EXTRA
    return pl.pallas_call(
        functools.partial(back_kernel, n),
        grid=(n // 2 + 1,),
        in_specs=[pl.BlockSpec(memory_space=pl.ANY)] + [whole(t) for t in (a_in, b_in, g, g_next)] + [pair] * 3
        + [whole(t) for t in tables],
        out_specs=[pair] * 4,
        out_shape=[shape] * 4,
        scratch_shapes=[pltpu.VMEM((n + 1, mz, ny), jnp.float32), pltpu.VMEM((mz, ny), jnp.float32),
                        pltpu.VMEM((2 * tall, ny), jnp.bfloat16), pltpu.VMEM((2 * tall, ny), jnp.bfloat16),
                        pltpu.VMEM((2, 2, tall, ny), jnp.float32), pltpu.SemaphoreType.DMA((n,))],
        compiler_params=pltpu.CompilerParams(dimension_semantics=("arbitrary",), vmem_limit_bytes=VMEM_LIMIT),
        name="back",
    )(a_loc, a_in, b_in, g, g_next, u, v, w, *tables)


def on_device(u, v, w):
    n, mz, ny = u.shape
    ngx, ngz = lax.axis_size("gx"), lax.axis_size("gz")
    u_lo, u_hi = shift_pair(u, "gx", 0)
    w_lo, w_hi = shift_pair(w, "gz", 1)
    a_loc, pay = front(u, v, w, u_lo, u_hi, w_lo, w_hi)
    ndev = ngx * ngz
    got = lax.all_to_all(pay.T.reshape(ndev, ny // ndev, -1), ("gx", "gz"), 0, 0)
    send = owner(got, ngx, ngz, n, mz, ny)
    ret = lax.all_to_all(send, ("gx", "gz"), 0, 0).reshape(ny, -1)
    return back(a_loc, ret, u, v, w)


def solution(mesh):
    spec = P("gx", "gz", None)
    return jax.shard_map(on_device, mesh=mesh, in_specs=(spec,) * 3, out_specs=(spec,) * 4, check_vma=False)
```

time: 2770 us -> 287 us (0.10)
  blocking collectives: 1180 us -> 42.3 us
  waiting for transfers between devices: 854 us -> 36.6 us
  matrix products: 280 us -> 16 us
  local copies, waits for them, and re-layouts: 243 us -> 19.2 us
  other arithmetic: 160 us -> 21.1 us
  Pallas kernels: 0 us -> 137 us
    all_to_all x3 -> x1, blocking collectives: 1180 us -> 42.3 us  [on_device(): ret = lax.all_to_all(send, ('gx', 'gz'), 0, 0).reshape(ny, -1)]
    all_to_all x3 -> x1, waiting for transfers between devices: 850 us -> 34 us  [on_device(): lax.all_to_all(pay.T.reshape(ndev, ny // ndev, -1), ('gx', 'gz'), 0, 0)]
    dot_general x6 -> x12, matrix products: 280 us -> 16 us  [the longest x2 4.47 us: owner(): jnp.einsum('djmx,mxq->djmq', even, t[..., :half], precision=HI)]
    all_to_all x8 -> x0, local copies, waits for them, and re-layouts: 145 us -> none  [the longest x2 40.1 us: on_device(): lax.all_to_all(cube.reshape(cx, cz * ny), 'gx', split_axis=1, concat_axis...]
    pallas_call x0 -> x2, Pallas kernels: none -> 137 us  [the longest x1 69.6 us: back(): pl.pallas_call(functools.partial(back_kernel, n), grid=(n // 2 + 1,), in_...]
    unnamed x1 -> x56, other arithmetic: 55.6 us -> 14.3 us
    add x3 -> x1, other arithmetic: 37.7 us -> 0.01 us  [owner(): rise = edge * jnp.exp(-theta[:, None, :] * (steps + 1.0))]
    dot_general x5 -> x0, other arithmetic: 28.7 us -> none  [the longest x1 9.17 us: on_device(): full = jnp.einsum('xky,ym->xkm', zspec, sine, precision=hi)]
  transfers between devices with their start and end apart: 11 -> 5, of which waited for: 5 -> 3; matrix products, arithmetic and copies ran while one was open for 2% -> 2% of each run, Pallas kernels for 0% -> 0%
where the time goes in v1:
time: 287 us; the launch traced here: 286 us
  Pallas kernels  137 us (48%)
  blocking collectives  42.3 us (15%)
  waiting for transfers between devices  36.6 us (13%)
  other arithmetic  21.1 us (7%)
  local copies, waits for them, and re-layouts  19.2 us (7%)
  matrix products  16 us (6%)
  starting transfers between devices  12.4 us (4%)
    pallas_call x1, Pallas kernels, back(): pl.pallas_call(functools.partial(back_kernel, n), grid=(n // 2 + 1,), in_...  69.6 us
    pallas_call x1, Pallas kernels, front(): pl.pallas_call(functools.partial(front_kernel, planes, steps), grid=(step...  67.2 us
    all_to_all x1, blocking collectives, on_device(): ret = lax.all_to_all(send, ('gx', 'gz'), 0, 0).reshape(ny, -1)  42.3 us
    all_to_all x1, waiting for transfers between devices, on_device(): lax.all_to_all(pay.T.reshape(ndev, ny // ndev, -1), ('gx', 'gz'), 0, 0)  34 us
    unnamed x56, other arithmetic  14.3 us
    all_to_all x1, starting transfers between devices, on_device(): lax.all_to_all(pay.T.reshape(ndev, ny // ndev, -1), ('gx', 'gz'), 0, 0)  8.2 us
  transfers between devices with their start and end apart: 5, of which 3 were waited for; matrix products, arithmetic and copies ran while one was open for 2% of the time, Pallas kernels for 0%

profile of v1, /device:TPU:1, one launch (start us, length us, event | category | flops | bytes accessed | tf_op | source)
XLA Modules:
  0.0 285.8 jit_solution(15279042842565139884)
XLA Ops:
  0.6 1.1 fusion.78
  1.8 2.6 collective-permute-start
  4.4 1.3 fusion.77
  5.7 1.3 collective-permute-start.3
  7.3 2.0 collective-permute-done.3
  12.7 67.2 %front.1 = (f32[32,192,768]{2,1,0:T(8,128)}, f32[480,768]{1,0:T(8,128)}) custom-call(bf16[1,192,768]{2,1,0:T(8,128)(2,1)} %copy-done.7, bf16[1,192,768]{2,1,0:T(8,128)(2,1)} %copy-done.6, bf16[32,192,768]{2,1,0:T(8,128)(2,1)} %u.3, bf16[32,192,768]{2,1,0:T(8,128)(2,1)} %u.3, bf16[32,192,768]{2,1,0:T(8,128)(2,1)} %u.3, bf16[32,192,768]{2,1,0:T(8,128)(2,1)} %v.3, ...), custom_call_target="tpu_custom_call" | custom-call | tf_op jit(solution)/shard_map/front/pallas_call | solution.py:244
  79.9 3.0 %copy.90 = f32[768,480]{1,0:T(8,128)} copy(f32[768,480]{0,1:T(8,128)} %bitcast.232) | data formatting | bytes 2949120 | tf_op jit(solution)/shard_map/transpose | solution.py:365
  82.9 8.2 %all-to-all-start = ((f32[32,24,480]{2,1,0:T(8,128)}), f32[32,24,480]{2,1,0:T(8,128)S(1)}, u32[]{:S(2)}, u32[]{:S(2)}) async-start(f32[32,24,480]{2,1,0:T(8,128)} %bitcast.1), calls=%async_computation | async-start | bytes 3145728 | tf_op jit(solution)/shard_map/all_to_all | solution.py:365
  93.8 34.0 %all-to-all-done = f32[32,24,480]{2,1,0:T(8,128)S(1)} async-done(((f32[32,24,480]{2,1,0:T(8,128)}), f32[32,24,480]{2,1,0:T(8,128)S(1)}, u32[]{:S(2)}, u32[]{:S(2)}) %all-to-all-start) | async-done | bytes 1474592 | tf_op jit(solution)/shard_map/all_to_all | solution.py:365
  129.8 0.8 fusion.13
  130.6 0.9 fusion.16
  131.5 0.9 fusion.1
  132.4 1.0 fusion.85
  134.1 1.5 convolution_bitcast_fusion
  135.6 0.9 copy.99
  136.5 1.2 dot_general.45
  137.7 2.0 convolution_divide_fusion
  142.5 1.8 reshape.281
  144.3 2.2 fusion.8
  146.5 2.2 fusion.10
  148.7 0.9 reshape.282
  149.6 1.6 fusion.4
  151.2 1.6 fusion.6
  158.6 0.8 constant_dynamic-update-slice_fusion.45
  160.3 0.8 constant_dynamic-update-slice_fusion.43
  161.9 0.8 constant_dynamic-update-slice_fusion.41
  163.6 0.8 constant_dynamic-update-slice_fusion.39
  165.3 0.8 constant_dynamic-update-slice_fusion.37
  169.6 0.9 constant_dynamic-update-slice_fusion.32
  171.4 42.3 %all_to_all.10 = f32[32,24,464]{2,1,0:T(8,128)S(1)} all-to-all(f32[32,24,464]{2,1,0:T(8,128)S(1)} %bitcast.225), channel_id=1, replica_groups=mesh['gx'=16,'gz'=2] {'gx','gz'}, dimensions={0} | all-to-all | bytes 2850816 | tf_op jit(solution)/shard_map/all_to_all | solution.py:367
  214.9 1.1 fusion.81
  216.0 69.6 %back.1 = (f32[32,192,768]{2,1,0:T(8,128)}, f32[32,192,768]{2,1,0:T(8,128)}, f32[32,192,768]{2,1,0:T(8,128)}, f32[32,192,768]{2,1,0:T(8,128)}) custom-call(f32[32,192,768]{2,1,0:T(8,128)} %get-tuple-element.6.a_hbm, f32[192,768]{1,0:T(8,128)} %get-tuple-element.77.a_in, f32[192,768]{1,0:T(8,128)} %get-tuple-element.76.b_in, f32[40,768]{1,0:T(8,128)} %get-tuple-element.75.g, ...), custom_call_target="tpu_custom_call" | custom-call | tf_op jit(solution)/shard_map/back/pallas_call | solution.py:343
  (150 shorter events, 26.2 us)
Async XLA Ops:
  1.7 9.5 %collective-permute-start.1 = (bf16[1,192,768]{2,1,0:T(8,128)(2,1)S(1)}, bf16[1,192,768]{2,1,0:T(8,128)(2,1)S(1)}, u32[]{:S(2)}, u32[]{:S(2)}) collective-permute-start(bf16[1,192,768]{2,1,0:T(8,128)(2,1)S(1)} %get-tuple-element.54), channel_id=1, source_target_pairs={{2,0},{4,2},{6,4},{8,6},{10,8},{12,10},{14,12},{16,14},{18,16},{20... | collective-permute-start | bytes 884744 | tf_op jit(solution)/shard_map/ppermute | solution.py:48
  1.8 9.4 %collective-permute-start = (bf16[1,192,768]{2,1,0:T(8,128)(2,1)S(1)}, bf16[1,192,768]{2,1,0:T(8,128)(2,1)S(1)}, u32[]{:S(2)}, u32[]{:S(2)}) collective-permute-start(bf16[1,192,768]{2,1,0:T(8,128)(2,1)S(1)} %get-tuple-element.55), channel_id=1, source_target_pairs={{0,2},{2,4},{4,6},{6,8},{8,10},{10,12},{12,14},{14,16},{16,18},{18... | collective-permute-start | bytes 884744 | tf_op jit(solution)/shard_map/ppermute | solution.py:47
  5.7 3.5 %collective-permute-start.3 = (bf16[32,1,768]{2,1,0:T(2,128)(2,1)S(1)}, bf16[32,1,768]{2,1,0:T(2,128)(2,1)S(1)}, u32[]{:S(2)}, u32[]{:S(2)}) collective-permute-start(bf16[32,1,768]{2,1,0:T(2,128)(2,1)S(1)} %get-tuple-element.52), channel_id=1, source_target_pairs={{1,0},{0,1},{3,2},{2,3},{5,4},{4,5},{7,6},{6,7},{9,8},{8,9},{11,10... | collective-permute-start | bytes 147464 | tf_op jit(solution)/shard_map/ppermute | solution.py:48
  7.0 3.5 %collective-permute-start.2 = (bf16[32,1,768]{2,1,0:T(2,128)(2,1)S(1)}, bf16[32,1,768]{2,1,0:T(2,128)(2,1)S(1)}, u32[]{:S(2)}, u32[]{:S(2)}) collective-permute-start(bf16[32,1,768]{2,1,0:T(2,128)(2,1)S(1)} %get-tuple-element.53), channel_id=1, source_target_pairs={{0,1},{1,0},{2,3},{3,2},{4,5},{5,4},{6,7},{7,6},{8,9},{9,8},{10,11... | collective-permute-start | bytes 147464 | tf_op jit(solution)/shard_map/ppermute | solution.py:47
  11.2 0.7 copy-start.6
  12.0 0.7 copy-start.7
  82.9 9.0 %copy-start.14 = (f32[192]{0:T(256)S(1)}, f32[192]{0:T(256)}, u32[]{:S(2)}) copy-start(f32[192]{0:T(256)} %constant.77.clone) | copy-start | bytes 2308
  82.9 9.0 %copy-start.15 = (f32[192]{0:T(256)S(1)}, f32[192]{0:T(256)}, u32[]{:S(2)}) copy-start(f32[192]{0:T(256)} %constant.76.clone) | copy-start | bytes 2308
  82.9 9.8 %copy-start.10 = (f32[512]{0:T(512)S(1)}, f32[512]{0:T(512)}, u32[]{:S(2)}) copy-start(f32[512]{0:T(512)} %constant.81.clone) | copy-start | bytes 6148
  82.9 10.6 %copy-start.13 = (f32[192]{0:T(256)S(1)}, f32[192]{0:T(256)}, u32[]{:S(2)}) copy-start(f32[192]{0:T(256)} %constant.78.clone) | copy-start | bytes 2308
  82.9 44.9 %all-to-all-start = ((f32[32,24,480]{2,1,0:T(8,128)}), f32[32,24,480]{2,1,0:T(8,128)S(1)}, u32[]{:S(2)}, u32[]{:S(2)}) async-start(f32[32,24,480]{2,1,0:T(8,128)} %bitcast.1), calls=%async_computation | async-start | bytes 3145728 | tf_op jit(solution)/shard_map/all_to_all | solution.py:365
  128.8 0.7 copy-start.9
  133.4 0.7 copy-start.12
  133.5 4.2 %copy-start.16 = (f32[2]{0:T(128)S(1)}, f32[2]{0:T(128)}, u32[]{:S(2)}) copy-start(f32[2]{0:T(128)} %constant.82.clone) | copy-start | bytes 28
  136.5 4.0 %copy-start.11 = (f32[2,2,1]{1,0,2:T(2,128)S(1)}, f32[2,2,1]{1,0,2:T(2,128)}, u32[]{:S(2)}) copy-start(f32[2,2,1]{1,0,2:T(2,128)} %constant.86) | copy-start | bytes 52
  137.6 2.1 copy-start.3
  141.0 13.9 %copy-start.1 = (f32[2,24,512]{2,1,0:T(8,128)}, f32[2,24,512]{2,1,0:T(8,128)S(1)}, u32[]{:S(2)}) copy-start(f32[2,24,512]{2,1,0:T(8,128)S(1)} %copy.104) | copy-start | bytes 294916
  149.6 3.1 %copy-start.8 = (f32[2,24,2]{2,1,0:T(8,128)S(1)}, f32[2,24,2]{2,1,0:T(8,128)}, u32[]{:S(2)}) copy-start(f32[2,24,2]{2,1,0:T(8,128)} %fusion.39) | copy-start | bytes 1156
  153.0 2.5 copy-start.5
  153.4 2.3 copy-start.4
  156.9 0.9 copy-start
  169.4 1.4 copy-start.2
  169.4 1.4 slice-start

commit v2 on v1

v2 whole, which is shorter than its diff:
```python
import functools
import math
import ml_dtypes
import numpy as np
import jax
import jax.numpy as jnp
from jax import lax
from jax.experimental import pallas as pl
from jax.experimental.pallas import tpu as pltpu
from jax.sharding import PartitionSpec as P

HI = lax.Precision.HIGHEST


def slab_order(count):
    return np.concatenate([np.arange(0, count, 2), np.arange(1, count, 2)])


def slab_table(count):
    order = slab_order(count)
    cell = np.arange(count)
    table = math.sqrt(2.0 / count) * np.sin(np.pi * np.outer(order, cell) / count)
    table[0, 0] = 1.0
    return table


def sine_table(count):
    index = np.arange(1, count + 1)
    angle = np.outer(index, index) % (2 * (count + 1)) * (np.pi / (count + 1))
    return math.sqrt(2.0 / (count + 1)) * np.sin(angle)


def hartley_table(count):
    index = np.arange(count)
    angle = np.outer(index, index) % count * (2.0 * np.pi / count)
    return np.cos(angle) + np.sin(angle)


def wall_part(count):
    return np.sin(np.arange(1, count + 1) * (np.pi / (2 * count + 2))) ** 2


def shift_pair(first, last, axis):
    count = lax.axis_size(axis)
    forward = [(i, (i + 1) % count) for i in range(count)]
    backward = [(target, source) for source, target in forward]
    return lax.ppermute(last, axis, forward), lax.ppermute(first, axis, backward)


VMEM_LIMIT = 60 * 1024 * 1024
EXTRA = 16


def split_np(table):
    wide = np.asarray(table, np.float32)
    high = wide.astype(ml_dtypes.bfloat16)
    low = (np.asarray(table, np.float64) - high.astype(np.float64)).astype(ml_dtypes.bfloat16)
    return jnp.asarray(high), jnp.asarray(low)


def split(value):
    high = value.astype(jnp.bfloat16)
    return high, (value - high.astype(jnp.float32)).astype(jnp.bfloat16)


def dot(a, b):
    return jnp.dot(a, b, preferred_element_type=jnp.float32)


def dot3(a, b):
    return dot(a[0], b[0]) + (dot(a[1], b[0]) + dot(a[0], b[1]))


def mode_planes(m_cells, ny):
    order = slab_order(m_cells)
    s = np.sqrt(np.sin(np.pi * order / (2 * m_cells))[:, None] ** 2 + wall_part(ny)[None])
    r = (np.sqrt(1 + s * s) - s) ** 2 * (order > 0)[:, None]
    edge = slab_table(m_cells)[:, 1] * (order > 0)
    edge = np.broadcast_to(edge[:, None], r.shape)
    return jnp.asarray(r, jnp.float32), jnp.asarray(edge, jnp.float32)


def round_up(count, unit=128):
    return -(-count // unit) * unit


def spans(mz, n):
    half, third = mz // 2, mz // 6
    return [(2 * mz, 2 * n), (0, third), (half, third), (mz, third), (mz + half, third)]


def width_of(mz, n):
    return 2 * mz + 2 * n + sum(size for _, size in spans(mz, n))


def pack(rows, mz, n):
    at = 2 * mz + 2 * n
    for start, size in spans(mz, n):
        value = rows[start:start + size, :]
        rows[at:at + size, :] = value - value.astype(jnp.bfloat16).astype(jnp.float32)
        at += size
    return rows[...].T.astype(jnp.bfloat16)


def unpack(rows, message, mz, n):
    rows[0:message.shape[1], :] = message[...].astype(jnp.float32).T
    at = 2 * mz + 2 * n
    for start, size in spans(mz, n):
        rows[start:start + size, :] = rows[start:start + size, :] + rows[at:at + size, :]
        at += size


def chunks(rows, size=24):
    half = rows // 2
    size = math.gcd(size, half)
    return [slice(i, i + size) for i in range(0, rows, size)]


def wall_gap(field):
    ny = field.shape[1]
    at = lax.broadcasted_iota(jnp.int32, field.shape, 1)
    after = jnp.where(at == ny - 1, 0.0, pltpu.roll(field, ny - 1, 1))
    before = jnp.where(at == 0, 0.0, pltpu.roll(field, 1, 1))
    return after - before


def front_kernel(planes, steps, u_lo, u_hi, u_prev, u, u_next, v, w, w_lo, w_hi, sh, sl, th, tl, r, edge,
                 a_out, pay_t, a_all, now, xa, xb, sa, sb, hits, pay, rims):
    i = pl.program_id(0)
    mz, ny = now.shape
    n = planes * steps
    half = mz // 2
    f = lambda t: t.astype(jnp.float32)

    def diverge(dst):
        row = lax.broadcasted_iota(jnp.int32, (mz, ny), 0)
        for p in range(planes):
            if p == 0:
                before = jnp.where(i == 0, f(u_lo[0]), f(u_prev[0]))
            else:
                before = f(u[p - 1])
            if p == planes - 1:
                after = jnp.where(i == steps - 1, f(u_hi[0]), f(u_next[0]))
            else:
                after = f(u[p + 1])
            mid = f(w[p])
            w_after = jnp.where(row == mz - 1, rims[1, pl.ds(i * planes + p, 1), :], pltpu.roll(mid, mz - 1, 0))
            w_before = jnp.where(row == 0, rims[0, pl.ds(i * planes + p, 1), :], pltpu.roll(mid, 1, 0))
            div = (after - before) + (w_after - w_before) + wall_gap(f(v[p]))
            high, low = split(div)
            dst[0, p * mz:(p + 1) * mz, :] = high
            dst[1, p * mz:(p + 1) * mz, :] = low

    def along_y(src, dst):
        lhs = jnp.concatenate([src[0], src[1], src[0]], axis=1)
        dst[...] = dot(lhs, jnp.concatenate([sh[...], sh[...], sl[...]], axis=0))

    def along_z(src):
        for p in range(planes):
            part = split(src[p * mz:(p + 1) * mz, :])
            right = jnp.concatenate([part[0], part[1], part[0]], axis=0)
            left = jnp.concatenate([th[...], th[...], tl[...]], axis=1)
            a = r[...] * now[...] + dot(left, right)
            now[...] = a
            a_out[p] = a
            a_all[(i - 2) * planes + p] = a

    xs, ss = (xa, xb), (sa, sb)

    @pl.when(i == 0)
    def _():
        now[...] = jnp.zeros_like(now)
        rims[0] = f(w_lo[...])
        rims[1] = f(w_hi[...])
        diverge(xa)

    @pl.when(i == 1)
    def _():
        along_y(xa, sa)
        diverge(xb)

    for par in range(2):
        @pl.when((i >= 2) & (i < steps) & (lax.rem(i, 2) == par))
        def _():
            along_y(xs[1 - par], ss[1 - par])
            diverge(xs[par])
            along_z(ss[par])

    @pl.when(i == steps)
    def _():
        along_y(xs[(steps - 1) % 2], ss[(steps - 1) % 2])
        along_z(ss[steps % 2])

    @pl.when(i == steps + 1)
    def _():
        along_z(ss[(steps + 1) % 2])
        pay[0:mz, :] = now[...]
        hits[...] = jnp.zeros_like(hits)
        for rows in chunks(mz, 16):
            rr = r[rows, :]
            ee = edge[rows, :]
            side = 0 if rows.start < half else 1
            start = -(rr * rr / (1.0 - rr * rr)) * now[rows, :]

            def body(k, part):
                x = n - 1 - k
                part = rr * (part - a_all[x, rows, :])
                add = ee * part
                total = add[0:8]
                for at in range(8, add.shape[0], 8):
                    total = total + add[at:at + 8]
                hits[side, x] = hits[side, x] + total
                return part

            part = lax.fori_loop(0, n, body, start, unroll=4)
            pay[mz + rows.start:mz + rows.stop, :] = -(1.0 - rr * rr) * part
        for x in range(n):
            pay[2 * mz + x:2 * mz + x + 1, :] = a_all[x, 0:1, :]
        t_e, t_o = jnp.sum(hits[0], axis=1), jnp.sum(hits[1], axis=1)
        pay[2 * mz:2 * mz + n, :] = pay[2 * mz:2 * mz + n, :] - (t_o + t_e)
        pay[2 * mz + n:2 * mz + 2 * n, :] = t_o - t_e
        pay_t[...] = pack(pay, mz, n)[:, 0:pay_t.shape[1]]


def front(u, v, w, u_lo, u_hi, w_lo, w_hi):
    n, mz, ny = u.shape
    planes = 2
    steps = n // planes
    r, edge = mode_planes(mz, ny)
    whole = lambda a: pl.BlockSpec(a.shape, lambda i: (0,) * a.ndim, pipeline_mode=pl.Buffered(1))
    here = lambda i: jnp.minimum(i, steps - 1)
    group = pl.BlockSpec((planes, mz, ny), lambda i: (here(i), 0, 0))
    tables = split_np(0.5 * sine_table(ny)) + split_np(slab_table(mz)) + (r, edge)
    prev = pl.BlockSpec((1, mz, ny), lambda i: (jnp.maximum(here(i) * planes - 1, 0), 0, 0))
    after = pl.BlockSpec((1, mz, ny), lambda i: (jnp.minimum(i * planes + planes, n - 1), 0, 0))
    rows = width_of(mz, n)
    return pl.pallas_call(
        functools.partial(front_kernel, planes, steps),
        grid=(steps + 2,),
        in_specs=[whole(u_lo), whole(u_hi), prev, group, after, group, group, whole(w_lo), whole(w_hi)] + [whole(t) for t in tables],
        out_specs=[pl.BlockSpec((planes, mz, ny), lambda i: (jnp.maximum(i - 2, 0), 0, 0)),
                   pl.BlockSpec((ny, rows), lambda i: (0, 0), pipeline_mode=pl.Buffered(1))],
        out_shape=[jax.ShapeDtypeStruct((n, mz, ny), jnp.float32), jax.ShapeDtypeStruct((ny, rows), jnp.bfloat16)],
        scratch_shapes=[pltpu.VMEM((n, mz, ny), jnp.float32), pltpu.VMEM((mz, ny), jnp.float32),
                        pltpu.VMEM((2, planes * mz, ny), jnp.bfloat16), pltpu.VMEM((2, planes * mz, ny), jnp.bfloat16),
                        pltpu.VMEM((planes * mz, ny), jnp.float32), pltpu.VMEM((planes * mz, ny), jnp.float32),
                        pltpu.VMEM((2, n, 8, ny), jnp.float32), pltpu.VMEM((round_up(rows), ny), jnp.float32),
                        pltpu.VMEM((2, n, ny), jnp.float32)],
        compiler_params=pltpu.CompilerParams(dimension_semantics=("arbitrary",), vmem_limit_bytes=VMEM_LIMIT),
        name="front",
    )(u_lo, u_hi, u, u, u, v, w, w_lo, w_hi, *tables)


def owner_kernel(ngx, ngz, n, recv, r, rn, wrap, gain, edge, first, last, inv, xh, xl, jh, jl,
                 out, buf, hits, mixed, res):
    mz, lanes = r.shape
    half = mz // 2
    mc = lanes // (ngx * ngz)
    step = ngz * mc
    unpack(buf, recv, mz, n)
    hits[...] = jnp.zeros_like(hits)

    def carries(up, down, rows):
        power = rn[rows, :]
        reach = 1
        while reach < ngx:
            up = up + power * pltpu.roll(up, step * reach, 1)
            down = down + power * pltpu.roll(down, lanes - step * reach, 1)
            reach *= 2
            if reach < ngx:
                power = power * power
        close = wrap[rows, :]
        return close * pltpu.roll(up, step, 1), close * pltpu.roll(down, lanes - step, 1)

    def fold(value):
        total = value[0:8]
        for at in range(8, value.shape[0], 8):
            total = total + value[at:at + 8]
        return total

    def below(rows):
        return slice(mz + rows.start, mz + rows.stop)

    for rows in chunks(mz, 16):
        up, down = carries(buf[rows, :], buf[below(rows), :], rows)
        res[rows, :] = gain[rows, :] * r[rows, :] * up
        res[below(rows), :] = gain[rows, :] * down
    for rows in chunks(mz, 32):
        rr = r[rows, :]
        side = 0 if rows.start < half else 1

        def rise(x, value):
            hits[0, side, x] = hits[0, side, x] + fold(value)
            return rr * value

        def fall(k, value):
            hits[1, side, n - 1 - k] = hits[1, side, n - 1 - k] + fold(value)
            return rr * value

        lax.fori_loop(0, n, rise, res[rows, :], unroll=4)
        lax.fori_loop(0, n, fall, res[below(rows), :], unroll=4)

    def beside(field, before):
        if ngz == 1:
            return field
        if before:
            return jnp.where(first[...] > 0.0, pltpu.roll(field, lanes - mc * (ngz - 1), 1), pltpu.roll(field, mc, 1))
        return jnp.where(last[...] > 0.0, pltpu.roll(field, mc * (ngz - 1), 1), pltpu.roll(field, lanes - mc, 1))

    t_e = jnp.sum(hits[0, 0] + hits[1, 0], axis=1)
    t_o = jnp.sum(hits[0, 1] + hits[1, 1], axis=1)
    own = buf[2 * mz:2 * mz + n, :] - (t_o + t_e)
    rhs = own - beside(buf[2 * mz + n:2 * mz + 2 * n, :] + (t_o - t_e), True)
    line = jnp.concatenate([rhs[:, d * step:(d + 1) * step] for d in range(ngx)], axis=0)
    across = (jh[...], jl[...])
    table = (xh[...], xl[...])
    line = dot3(split(line), across)
    line = dot3(table, split(line)) * inv[...]
    line = dot3(table, split(line))
    line = dot3(split(line), across)
    g = jnp.concatenate([line[d * n:(d + 1) * n] for d in range(ngx)], axis=1)
    g_next = beside(g, False)
    mixed[0] = g - g_next
    mixed[1] = g + g_next
    res[2 * mz:2 * mz + n, :] = g
    res[2 * mz + n:2 * mz + 2 * n, :] = g_next
    for rows in chunks(mz, 32):
        rr = r[rows, :]
        side = 0 if rows.start < half else 1
        zero = jnp.zeros_like(rr)
        up = lax.fori_loop(0, n, lambda x, t: rr * t + mixed[side, pl.ds(x, 1), :], zero, unroll=4)
        buf[rows, :] = buf[rows, :] - edge[rows, :] * up
        down = lax.fori_loop(0, n, lambda k, t: rr * (t + mixed[side, pl.ds(n - 1 - k, 1), :]), zero, unroll=4)
        buf[below(rows), :] = buf[below(rows), :] - edge[rows, :] * down
    for rows in chunks(mz, 16):
        up, down = carries(buf[rows, :], buf[below(rows), :], rows)
        res[rows, :] = up
        res[below(rows), :] = down
    res[0:1, :] = pltpu.roll(g[n - 1:n], step, 1)
    res[mz:mz + 1, :] = pltpu.roll(g[0:1], lanes - step, 1)
    out[...] = pack(res, mz, n)[:, 0:out.shape[1]]


def owner_tables(ngx, ngz, n, mz, ny):
    nx, ndev = ngx * n, ngx * ngz
    mc = ny // ndev
    start = (lax.axis_index("gx") * ngz + lax.axis_index("gz")) * mc
    order = slab_order(mz)
    wall = lax.dynamic_slice_in_dim(jnp.asarray(wall_part(ny), jnp.float32), start, mc)
    across = jnp.asarray(np.sin(np.pi * order / (2 * mz)) ** 2, jnp.float32)[:, None]
    real = jnp.asarray(order > 0, jnp.float32)[:, None]
    s = jnp.sqrt(wall + across)
    theta = 2.0 * jnp.log1p(s + s * s / (1.0 + jnp.sqrt(1.0 + s * s)))
    wide = lambda t: jnp.tile(t * real, (1, ndev))
    one = jnp.exp(-theta)
    edge = jnp.asarray(slab_table(mz)[:, 1:2], jnp.float32)
    r, rn = wide(one), wide(jnp.exp(-float(n) * theta))
    wrap = wide(1.0 / (1.0 - jnp.exp(-float(nx) * theta)))
    gain = wide(-edge * one / (1.0 - one * one))
    s2 = wall + jnp.asarray(np.sin(np.pi * np.arange(nx) / nx) ** 2, jnp.float32)[:, None]
    sq, root = jnp.sqrt(s2), jnp.sqrt(1.0 + s2)
    decay = jnp.exp(-2.0 * mz * jnp.log1p(sq + s2 / (1.0 + root)))
    inv = []
    for j in range(ngz):
        bend = 1.0 + decay * decay - 2.0 * math.cos(2.0 * math.pi * j / ngz) * decay
        inv.append(-(1.0 - decay * decay) / (4.0 * float(nx * ngz) * sq * root * bend))
    slab = np.arange(ny) // mc % ngz
    first = jnp.asarray((slab == 0)[None], jnp.float32)
    last = jnp.asarray((slab == ngz - 1)[None], jnp.float32)
    edge = mode_planes(mz, ny)[1]
    sides = split_np(hartley_table(nx)) + split_np(np.kron(hartley_table(ngz), np.eye(mc)))
    return (r, rn, wrap, gain, edge, first, last, jnp.concatenate(inv, axis=1)) + sides


def owner(recv, tables, ngx, ngz, n, mz):
    ny, width = recv.shape
    return pl.pallas_call(
        functools.partial(owner_kernel, ngx, ngz, n),
        out_shape=jax.ShapeDtypeStruct((ny, width), jnp.bfloat16),
        scratch_shapes=[pltpu.VMEM((round_up(width), ny), jnp.float32), pltpu.VMEM((2, 2, n, 8, ny), jnp.float32),
                        pltpu.VMEM((2, n, ny), jnp.float32), pltpu.VMEM((round_up(width), ny), jnp.float32)],
        compiler_params=pltpu.CompilerParams(vmem_limit_bytes=VMEM_LIMIT),
        name="owner",
    )(recv, *tables)


def back_kernel(n, a_hbm, ret, u, v, w, sh, sl, th, tl, r, edge, stiff,
                p_out, u_out, v_out, w_out, a_all, now, xa, xb, pa, pb, rt, rims, sems):
    s = pl.program_id(0)
    mz, ny = now.shape
    half = mz // 2
    tall = mz + EXTRA
    last = n // 2
    f = lambda a: a.astype(jnp.float32)
    line = lambda x: rims[pl.ds(x + 2, 1), :]
    line_next = lambda x: rt[pl.ds(2 * mz + n + jnp.clip(x, 0, n - 1), 1), :]

    def sweep():
        copies = [pltpu.make_async_copy(a_hbm.at[x], a_all.at[x + 1], sems.at[x]) for x in range(n)]
        for copy in copies:
            copy.start()
        unpack(rt, ret, mz, n)
        rims[...] = jnp.zeros_like(rims)
        rims[1:2, :] = rt[0:1, :]
        rims[2:2 + n, :] = rt[2 * mz:2 * mz + n, :]
        rims[2 + n:3 + n, :] = rt[mz:mz + 1, :]
        now[...] = rt[0:mz, :]
        a_all[0] = rt[0:mz, :]

        def body(x, carry):
            pltpu.make_async_copy(a_hbm.at[x], a_all.at[x + 1], sems.at[x]).wait()
            here, there = line(x), line_next(x)
            for rows in chunks(mz):
                mix = here - there if rows.start < half else here + there
                new = r[rows, :] * now[rows, :] - edge[rows, :] * mix
                now[rows, :] = new
                a_all[x + 1, rows, :] = a_all[x + 1, rows, :] + new
            return carry

        lax.fori_loop(0, n, body, 0)
        for rows in chunks(mz):
            rr = r[rows, :]
            b_in = rt[mz + rows.start:mz + rows.stop, :]
            now[rows, :] = -(rr * rr * a_all[n, rows, :] + b_in) / (1.0 - rr * rr)

    def along_z(dst, begin):
        for t in range(2):
            x = n - 2 * s - t
            if not (begin and t == 0):
                now[...] = r[...] * (now[...] - a_all[x + 1])
            now[0:1, :] = line(x)
            hat = split(now[...])
            now[0:1, :] = jnp.zeros((1, ny), jnp.float32)
            left = jnp.concatenate([th[...], th[...], tl[...]], axis=1)
            pz = dot(left, jnp.concatenate([hat[0], hat[1], hat[0]], axis=0))
            high, low = split(pz)
            base = t * tall
            dst[0, base:base + mz, :] = high
            dst[1, base:base + mz, :] = low
            under = (a_all[jnp.minimum(x + 1, n), 0:1, :] - pz[1:2, :] - line(x + 1) - line(x - 1)
                     + stiff[...] * line(x))
            at = lax.broadcasted_iota(jnp.int32, (EXTRA, ny), 0)
            extra = jnp.where(at == 0, line_next(x), jnp.where(at == EXTRA - 1, under, 0.0))
            high, low = split(extra)
            dst[0, base + mz:base + tall, :] = high
            dst[1, base + mz:base + tall, :] = low

    def along_y(src, dst):
        lhs = jnp.concatenate([src[0], src[1], src[0]], axis=1)
        fresh = dot(lhs, jnp.concatenate([sh[...], sh[...], sl[...]], axis=0))
        for t in range(2):
            dst[t] = fresh[t * tall:(t + 1) * tall]

    def finish(old, new):
        trio = ((1, old[0, :mz], old[1], new[0, :mz]), (0, old[1, :mz], new[0], new[1, :mz]))
        for k, after, full, before in trio:
            mid = full[:mz]
            p_out[k] = mid
            u_out[k] = f(u[k]) - 0.5 * (after - before)
            v_out[k] = f(v[k]) - 0.5 * wall_gap(mid)
            up, down = pltpu.roll(full, tall - 1, 0)[:mz], pltpu.roll(full, 1, 0)[:mz]
            w_out[k] = f(w[k]) - 0.5 * (up - down)

    xs, ps = (xa, xb), (pa, pb)

    @pl.when(s == 0)
    def _():
        sweep()
        along_z(xa, True)

    @pl.when(s == 1)
    def _():
        along_y(xa, pa)
        along_z(xb, False)

    for par in range(2):
        @pl.when((s >= 2) & (s <= last) & (lax.rem(s, 2) == par))
        def _():
            along_y(xs[1 - par], ps[1 - par])
            along_z(xs[par], False)
            finish(ps[par], ps[1 - par])

    @pl.when(s == last + 1)
    def _():
        along_y(xs[last % 2], ps[last % 2])
        finish(ps[1 - last % 2], ps[last % 2])


def back(a_loc, ret, u, v, w):
    n, mz, ny = u.shape
    r, edge = mode_planes(mz, ny)
    stiff = jnp.asarray(4.0 + 4.0 * wall_part(ny)[None], jnp.float32)
    tables = split_np(sine_table(ny)) + split_np(slab_table(mz).T) + (r, edge, stiff)
    whole = lambda a: pl.BlockSpec(a.shape, lambda i: (0,) * a.ndim, pipeline_mode=pl.Buffered(1))
    pair = pl.BlockSpec((2, mz, ny), lambda s: (jnp.clip(n // 2 + 1 - s, 0, n // 2 - 1), 0, 0))
    shape = jax.ShapeDtypeStruct((n, mz, ny), jnp.float32)
    tall = mz + EXTRA
    return pl.pallas_call(
        functools.partial(back_kernel, n),
        grid=(n // 2 + 2,),
        in_specs=[pl.BlockSpec(memory_space=pl.ANY), whole(ret)] + [pair] * 3 + [whole(t) for t in tables],
        out_specs=[pair] * 4,
        out_shape=[shape] * 4,
        scratch_shapes=[pltpu.VMEM((n + 1, mz, ny), jnp.float32), pltpu.VMEM((mz, ny), jnp.float32),
                        pltpu.VMEM((2, 2 * tall, ny), jnp.bfloat16), pltpu.VMEM((2, 2 * tall, ny), jnp.bfloat16),
                        pltpu.VMEM((2, tall, ny), jnp.float32), pltpu.VMEM((2, tall, ny), jnp.float32),
                        pltpu.VMEM((round_up(ret.shape[1]), ny), jnp.float32), pltpu.VMEM((n + 8, ny), jnp.float32),
                        pltpu.SemaphoreType.DMA((n,))],
        compiler_params=pltpu.CompilerParams(dimension_semantics=("arbitrary",), vmem_limit_bytes=VMEM_LIMIT),
        name="back",
    )(a_loc, ret, u, v, w, *tables)


def on_device(u, v, w):
    n, mz, ny = u.shape
    ngx, ngz = lax.axis_size("gx"), lax.axis_size("gz")
    ndev = ngx * ngz
    tables = owner_tables(ngx, ngz, n, mz, ny)
    w_lo, w_hi = shift_pair(w[:, 0], w[:, -1], "gz")
    u_lo, u_hi = shift_pair(u[:1], u[-1:], "gx")
    a_loc, pay = front(u, v, w, u_lo, u_hi, w_lo, w_hi)

    def swap(message):
        parts = message.reshape(ndev, ny // ndev, -1)
        return lax.all_to_all(parts, ("gx", "gz"), 0, 0).reshape(ny, -1)

    ret = swap(owner(swap(pay), tables, ngx, ngz, n, mz))
    return back(a_loc, ret, u, v, w)


def solution(mesh):
    spec = P("gx", "gz", None)
    return jax.shard_map(on_device, mesh=mesh, in_specs=(spec,) * 3, out_specs=(spec,) * 4, check_vma=False)
```

time: 287 us -> 205 us (0.71)
  other arithmetic: 21.1 us -> 0.3 us
  matrix products: 16 us -> 0 us
  waiting for transfers between devices: 36.6 us -> 22.2 us
  blocking collectives: 42.3 us -> 28.5 us
  local copies, waits for them, and re-layouts: 19.2 us -> 10.2 us
  Pallas kernels: 137 us -> 130 us
    dot_general x12 -> x0, matrix products: 16 us -> none  [the longest x2 4.47 us: owner(): jnp.einsum('djmx,mxq->djmq', even, t[..., :half], precision=HI)]
    all_to_all x1, waiting for transfers between devices: 34 us -> 18.4 us  [swap(): return lax.all_to_all(parts, ('gx', 'gz'), 0, 0).reshape(ny, -1)]
    unnamed x56 -> x0, other arithmetic: 14.3 us -> none
    pallas_call x1, Pallas kernels: 67.2 us -> 53.4 us  [front(): pl.pallas_call(functools.partial(front_kernel, planes, steps), grid=(step...]
    all_to_all x1, blocking collectives: 42.3 us -> 28.5 us  [swap(): return lax.all_to_all(parts, ('gx', 'gz'), 0, 0).reshape(ny, -1)]
    pallas_call x1 -> x2, Pallas kernels: 69.6 us -> 77 us  [the longest x1 56.4 us: back(): pl.pallas_call(functools.partial(back_kernel, n), grid=(n // 2 + 2,), in_...]
    another operation x2 -> x8, local copies, waits for them, and re-layouts: 0.01 us -> 4.47 us  [owner_tables(): wide = lambda t: jnp.tile(t * real, (1, ndev))]
    transpose x2 -> x0, local copies, waits for them, and re-layouts: 3.86 us -> none  [the longest x1 2.99 us: on_device(): pay.T.reshape(ndev, ny // ndev, -1)]
  transfers between devices with their start and end apart: 5 -> 5, of which waited for: 3 -> 4; matrix products, arithmetic and copies ran while one was open for 2% -> 4% of each run, Pallas kernels for 0% -> 0%
where the time goes in v2:
time: 205 us; the launch traced here: 204 us
  Pallas kernels  130 us (63%)
  blocking collectives  28.5 us (14%)
  waiting for transfers between devices  22.2 us (11%)
  starting transfers between devices  11.6 us (6%)
  local copies, waits for them, and re-layouts  10.2 us (5%)
    pallas_call x1, Pallas kernels, back(): pl.pallas_call(functools.partial(back_kernel, n), grid=(n // 2 + 2,), in_...  56.4 us
    pallas_call x1, Pallas kernels, front(): pl.pallas_call(functools.partial(front_kernel, planes, steps), grid=(step...  53.4 us
    all_to_all x1, blocking collectives, swap(): return lax.all_to_all(parts, ('gx', 'gz'), 0, 0).reshape(ny, -1)  28.5 us
    pallas_call x1, Pallas kernels, owner(): pl.pallas_call(functools.partial(owner_kernel, ngx, ngz, n), out_shape=ja...  20.6 us
    all_to_all x1, waiting for transfers between devices, swap(): return lax.all_to_all(parts, ('gx', 'gz'), 0, 0).reshape(ny, -1)  18.4 us
    all_to_all x1, starting transfers between devices, swap(): return lax.all_to_all(parts, ('gx', 'gz'), 0, 0).reshape(ny, -1)  7.33 us
    another operation x8, local copies, waits for them, and re-layouts, owner_tables(): wide = lambda t: jnp.tile(t * real, (1, ndev))  4.47 us
  transfers between devices with their start and end apart: 5, of which 4 were waited for; matrix products, arithmetic and copies ran while one was open for 4% of the time, Pallas kernels for 0%

profile of v2, /device:TPU:1, one launch (start us, length us, event | category | flops | bytes accessed | tf_op | source)
XLA Modules:
  0.0 204.1 jit_solution(11700747189085339416)
XLA Ops:
  0.6 1.1 fusion.14
  1.7 0.1 collective-permute-start.1
  1.8 2.6 %collective-permute-start = (bf16[1,192,768]{2,1,0:T(8,128)(2,1)S(1)}, bf16[1,192,768]{2,1,0:T(8,128)(2,1)S(1)}, u32[]{:S(2)}, u32[]{:S(2)}) collective-permute-start(bf16[1,192,768]{2,1,0:T(8,128)(2,1)S(1)} %get-tuple-element.11), channel_id=1, source_target_pairs={{0,2},{2,4},{4,6},{6,8},{8,10},{10,12},{12,14},{14,16},{16,18},{18... | collective-permute-start | bytes 884744 | tf_op jit(solution)/shard_map/ppermute | solution.py:47
  4.4 1.3 fusion.13
  5.7 1.3 collective-permute-start.2
  7.1 0.0 copy-start.5
  7.1 0.0 copy-start.6
  7.1 0.0 copy-start.7
  7.1 0.3 collective-permute-start.3
  7.4 1.3 collective-permute-done.2.w_lo
  8.7 1.4 collective-permute-done.3.w_hi
  10.1 1.2 collective-permute-done.u_lo
  11.3 0.7 copy-done.2
  12.0 53.4 %front.1 = (f32[32,192,768]{2,1,0:T(8,128)}, bf16[768,640]{1,0:T(8,128)(2,1)}) custom-call(bf16[1,192,768]{2,1,0:T(8,128)(2,1)} %copy-done.2, bf16[1,192,768]{2,1,0:T(8,128)(2,1)} %copy-done.1, bf16[32,192,768]{2,1,0:T(8,128)(2,1)} %u.3, bf16[32,192,768]{2,1,0:T(8,128)(2,1)} %u.3, bf16[32,192,768]{2,1,0:T(8,128)(2,1)} %u.3, bf16[32,192,768]{2,1,0:T(8,128)(2,1)} %v.3, ...), custom_call_target="tpu_custom_call" | custom-call | tf_op jit(solution)/shard_map/front/pallas_call | solution.py:237
  65.4 7.3 %all-to-all-start = ((bf16[32,24,640]{2,1,0:T(8,128)(2,1)}), bf16[32,24,640]{2,1,0:T(8,128)(2,1)S(1)}, u32[]{:S(2)}, u32[]{:S(2)}) async-start(bf16[32,24,640]{2,1,0:T(8,128)(2,1)} %bitcast.21), calls=%async_computation | async-start | bytes 1966080 | tf_op jit(solution)/shard_map/all_to_all | solution.py:525
  72.7 0.8 dynamic_slice.3
  73.5 0.2 fusion.10
  73.7 0.9 copy.46.inv
  74.5 0.1 divide_multiply_fusion
  74.7 0.1 tile.42
  74.7 1.1 copy.45.gain
  75.8 0.1 tile.18
  75.8 1.1 copy.43.rn
  76.9 0.1 tile.40
  77.0 1.1 copy.44.wrap
  78.0 0.1 tile.16
  78.1 1.1 copy.42.r
  79.2 18.4 %all-to-all-done = bf16[32,24,640]{2,1,0:T(8,128)(2,1)S(1)} async-done(((bf16[32,24,640]{2,1,0:T(8,128)(2,1)}), bf16[32,24,640]{2,1,0:T(8,128)(2,1)S(1)}, u32[]{:S(2)}, u32[]{:S(2)}) %all-to-all-start) | async-done | bytes 983072 | tf_op jit(solution)/shard_map/all_to_all | solution.py:525
  97.5 0.9 copy-done
  98.4 20.6 %owner.1 = bf16[768,640]{1,0:T(8,128)(2,1)} custom-call(bf16[768,640]{1,0:T(8,128)(2,1)} %bitcast.14, f32[192,768]{1,0:T(8,128)} %copy.42.r, f32[192,768]{1,0:T(8,128)} %copy.43.rn, f32[192,768]{1,0:T(8,128)} %copy.44.wrap, f32[192,768]{1,0:T(8,128)} %copy.45.gain, f32[192,768]{1,0:T(8,128)} %constant.85.clone.edge, f32[1,768]{1,0:T(1,128)} %constant.83.clone.first, ...), custom_call_target="tpu_custom_call" | custom-call | tf_op jit(solution)/shard_map/owner/pallas_call | solution.py:377
  119.1 28.5 %all_to_all.10 = bf16[32,24,640]{2,1,0:T(8,128)(2,1)} all-to-all(bf16[32,24,640]{2,1,0:T(8,128)(2,1)} %bitcast.15), channel_id=1, replica_groups=mesh['gx'=16,'gz'=2] {'gx','gz'}, dimensions={0} | all-to-all | bytes 1966080 | tf_op jit(solution)/shard_map/all_to_all | solution.py:525
  147.6 56.4 %back.1 = (f32[32,192,768]{2,1,0:T(8,128)}, f32[32,192,768]{2,1,0:T(8,128)}, f32[32,192,768]{2,1,0:T(8,128)}, f32[32,192,768]{2,1,0:T(8,128)}) custom-call(f32[32,192,768]{2,1,0:T(8,128)} %get-tuple-element.6.a_hbm, bf16[768,640]{1,0:T(8,128)(2,1)} %bitcast.16, bf16[32,192,768]{2,1,0:T(8,128)(2,1)} %u.3, bf16[32,192,768]{2,1,0:T(8,128)(2,1)} %v.3, ...), custom_call_target="tpu_custom_call" | custom-call | tf_op jit(solution)/shard_map/back/pallas_call | solution.py:498
  (17 shorter events, 0.1 us)
Async XLA Ops:
  1.7 8.4 %collective-permute-start.1 = (bf16[1,192,768]{2,1,0:T(8,128)(2,1)S(1)}, bf16[1,192,768]{2,1,0:T(8,128)(2,1)S(1)}, u32[]{:S(2)}, u32[]{:S(2)}) collective-permute-start(bf16[1,192,768]{2,1,0:T(8,128)(2,1)S(1)} %get-tuple-element.10), channel_id=1, source_target_pairs={{2,0},{4,2},{6,4},{8,6},{10,8},{12,10},{14,12},{16,14},{18,16},{20... | collective-permute-start | bytes 884744 | tf_op jit(solution)/shard_map/ppermute | solution.py:47
  1.8 9.4 %collective-permute-start = (bf16[1,192,768]{2,1,0:T(8,128)(2,1)S(1)}, bf16[1,192,768]{2,1,0:T(8,128)(2,1)S(1)}, u32[]{:S(2)}, u32[]{:S(2)}) collective-permute-start(bf16[1,192,768]{2,1,0:T(8,128)(2,1)S(1)} %get-tuple-element.11), channel_id=1, source_target_pairs={{0,2},{2,4},{4,6},{6,8},{8,10},{10,12},{12,14},{14,16},{16,18},{18... | collective-permute-start | bytes 884744 | tf_op jit(solution)/shard_map/ppermute | solution.py:47
  5.7 3.0 %collective-permute-start.2 = (bf16[32,768]{1,0:T(8,128)(2,1)S(1)}, bf16[32,768]{1,0:T(8,128)(2,1)S(1)}, u32[]{:S(2)}, u32[]{:S(2)}) collective-permute-start(bf16[32,768]{1,0:T(8,128)(2,1)S(1)} %bitcast.22), channel_id=1, source_target_pairs={{0,1},{1,0},{2,3},{3,2},{4,5},{5,4},{6,7},{7,6},{8,9},{9,8},{10,11... | collective-permute-start | bytes 147464 | tf_op jit(solution)/shard_map/ppermute | solution.py:47
  7.1 66.4 %copy-start.5 = (f32[512]{0:T(512)S(1)}, f32[512]{0:T(512)}, u32[]{:S(2)}) copy-start(f32[512]{0:T(512)} %constant.82.clone) | copy-start | bytes 6148
  7.1 67.5 %copy-start.6 = (f32[192]{0:T(256)S(1)}, f32[192]{0:T(256)}, u32[]{:S(2)}) copy-start(f32[192]{0:T(256)} %constant.101) | copy-start | bytes 2308
  7.1 67.4 %copy-start.7 = (f32[192]{0:T(256)S(1)}, f32[192]{0:T(256)}, u32[]{:S(2)}) copy-start(f32[192]{0:T(256)} %constant.80.clone) | copy-start | bytes 2308
  7.1 67.4 %copy-start.8 = (f32[192]{0:T(256)S(1)}, f32[192]{0:T(256)}, u32[]{:S(2)}) copy-start(f32[192]{0:T(256)} %constant.79.clone) | copy-start | bytes 2308
  7.1 3.0 %collective-permute-start.3 = (bf16[32,768]{1,0:T(8,128)(2,1)S(1)}, bf16[32,768]{1,0:T(8,128)(2,1)S(1)}, u32[]{:S(2)}, u32[]{:S(2)}) collective-permute-start(bf16[32,768]{1,0:T(8,128)(2,1)S(1)} %bitcast.23), channel_id=1, source_target_pairs={{1,0},{0,1},{3,2},{2,3},{5,4},{4,5},{7,6},{6,7},{9,8},{8,9},{11,10... | collective-permute-start | bytes 147464 | tf_op jit(solution)/shard_map/ppermute | solution.py:47
  8.7 2.5 %copy-start.3 = (bf16[32,768]{1,0:T(8,128)(2,1)}, bf16[32,768]{1,0:T(8,128)(2,1)S(1)}, u32[]{:S(2)}) copy-start(bf16[32,768]{1,0:T(8,128)(2,1)S(1)} %collective-permute-done.2.w_lo) | copy-start | bytes 147460
  10.1 1.2 copy-start.4
  10.1 1.2 copy-start.1
  11.3 0.7 copy-start.2
  65.4 32.1 %all-to-all-start = ((bf16[32,24,640]{2,1,0:T(8,128)(2,1)}), bf16[32,24,640]{2,1,0:T(8,128)(2,1)S(1)}, u32[]{:S(2)}, u32[]{:S(2)}) async-start(bf16[32,24,640]{2,1,0:T(8,128)(2,1)} %bitcast.21), calls=%async_computation | async-start | bytes 1966080 | tf_op jit(solution)/shard_map/all_to_all | solution.py:525
  97.5 0.9 copy-start

commit v3 on v2

--- a/solution.py
+++ b/solution.py
@@ -36,8 +36,22 @@
     return np.cos(angle) + np.sin(angle)
 
 
-def wall_part(count):
-    return np.sin(np.arange(1, count + 1) * (np.pi / (2 * count + 2))) ** 2
+def wall_order(count, owners):
+    places, each, third = np.arange(count // 2), count // owners, count // owners // 3
+    owner, slot = places // each, places % each
+    low = owner * third + slot
+    high = count // 6 + owner * 2 * third + slot - third
+    rank = np.where(slot < third, low, high)
+    return np.concatenate([2 * rank, 2 * rank + 1])
+
+
+def wall_part(count, owners):
+    return np.sin((wall_order(count, owners) + 1) * (np.pi / (2 * count + 2))) ** 2
+
+
+def folded_tables(count, owners, scale):
+    table = scale * sine_table(count)[:count // 2, wall_order(count, owners)]
+    return split_np(table[:, :count // 2]) + split_np(table[:, count // 2:])
 
 
 def shift_pair(first, last, axis):
@@ -71,9 +85,9 @@
     return dot(a[0], b[0]) + (dot(a[1], b[0]) + dot(a[0], b[1]))
 
 
-def mode_planes(m_cells, ny):
+def mode_planes(m_cells, ny, owners):
     order = slab_order(m_cells)
-    s = np.sqrt(np.sin(np.pi * order / (2 * m_cells))[:, None] ** 2 + wall_part(ny)[None])
+    s = np.sqrt(np.sin(np.pi * order / (2 * m_cells))[:, None] ** 2 + wall_part(ny, owners)[None])
     r = (np.sqrt(1 + s * s) - s) ** 2 * (order > 0)[:, None]
     edge = slab_table(m_cells)[:, 1] * (order > 0)
     edge = np.broadcast_to(edge[:, None], r.shape)
@@ -89,24 +103,45 @@
     return [(2 * mz, 2 * n), (0, third), (half, third), (mz, third), (mz + half, third)]
 
 
+def piece_of(mz, n):
+    return -(-sum(size for _, size in spans(mz, n)) // 24) * 8
+
+
 def width_of(mz, n):
-    return 2 * mz + 2 * n + sum(size for _, size in spans(mz, n))
-
-
-def pack(rows, mz, n):
-    at = 2 * mz + 2 * n
+    return 2 * mz + 2 * n + piece_of(mz, n)
+
+
+def slot_third(shape, mc):
+    lane = lax.broadcasted_iota(jnp.int32, shape, 1)
+    return lax.div(lax.rem(lane, mc), mc // 3)
+
+
+def pack(rows, low, mz, n, mc):
+    at, main, piece = 0, 2 * mz + 2 * n, piece_of(mz, n)
+    lanes = rows.shape[1]
+    low[...] = jnp.zeros_like(low)
     for start, size in spans(mz, n):
         value = rows[start:start + size, :]
-        rows[at:at + size, :] = value - value.astype(jnp.bfloat16).astype(jnp.float32)
+        low[at:at + size, :] = value - value.astype(jnp.bfloat16).astype(jnp.float32)
         at += size
+    third = slot_third((piece, lanes), mc)
+    mix = jnp.where(third == 1, pltpu.roll(low[piece:2 * piece, :], mc // 3, 1), low[0:piece, :])
+    mix = jnp.where(third == 2, pltpu.roll(low[2 * piece:3 * piece, :], mc // 3 * 2, 1), mix)
+    rows[main:main + piece, :] = mix
     return rows[...].T.astype(jnp.bfloat16)
 
 
-def unpack(rows, message, mz, n):
+def unpack(rows, low, message, mz, n, mc):
+    at, main, piece = 0, 2 * mz + 2 * n, piece_of(mz, n)
+    lanes = rows.shape[1]
     rows[0:message.shape[1], :] = message[...].astype(jnp.float32).T
-    at = 2 * mz + 2 * n
+    first = slot_third((piece, lanes), mc) == 0
+    mix = rows[main:main + piece, :]
+    for k in range(3):
+        moved = pltpu.roll(mix, lanes - k * (mc // 3), 1) if k else mix
+        low[k * piece:(k + 1) * piece, :] = jnp.where(first, moved, 0.0)
     for start, size in spans(mz, n):
-        rows[start:start + size, :] = rows[start:start + size, :] + rows[at:at + size, :]
+        rows[start:start + size, :] = rows[start:start + size, :] + low[at:at + size, :]
         at += size
 
 
@@ -114,6 +149,23 @@
     half = rows // 2
     size = math.gcd(size, half)
     return [slice(i, i + size) for i in range(0, rows, size)]
+
+
+def flip(field):
+    rows, width = field.shape
+    if width % 128:
+        return jnp.flip(field, 1)
+    at = 127 - lax.broadcasted_iota(jnp.int32, (rows, 128), 1)
+    parts = [jnp.take_along_axis(field[:, k:k + 128], at, axis=1) for k in range(0, width, 128)]
+    return jnp.concatenate(parts[::-1], axis=1)
+
+
+def fold_dot(src, tables, out):
+    middle = out.shape[1] // 2
+    for k, (high, low) in enumerate((tables[:2], tables[2:])):
+        cols = slice(k * middle, (k + 1) * middle)
+        lhs = jnp.concatenate([src[0, :, cols], src[1, :, cols], src[0, :, cols]], axis=1)
+        out[:, cols] = dot(lhs, jnp.concatenate([high[...], high[...], low[...]], axis=0))
 
 
 def wall_gap(field):
@@ -124,8 +176,8 @@
     return after - before
 
 
-def front_kernel(planes, steps, u_lo, u_hi, u_prev, u, u_next, v, w, w_lo, w_hi, sh, sl, th, tl, r, edge,
-                 a_out, pay_t, a_all, now, xa, xb, sa, sb, hits, pay, rims):
+def front_kernel(planes, steps, mc, u_lo, u_hi, u_prev, u, u_next, v, w, w_lo, w_hi, eh, el, oh, ol, th, tl, r, edge,
+                 a_out, pay_t, a_all, now, xa, xb, sa, sb, hits, pay, low, rims):
     i = pl.program_id(0)
     mz, ny = now.shape
     n = planes * steps
@@ -147,13 +199,14 @@
             w_after = jnp.where(row == mz - 1, rims[1, pl.ds(i * planes + p, 1), :], pltpu.roll(mid, mz - 1, 0))
             w_before = jnp.where(row == 0, rims[0, pl.ds(i * planes + p, 1), :], pltpu.roll(mid, 1, 0))
             div = (after - before) + (w_after - w_before) + wall_gap(f(v[p]))
-            high, low = split(div)
-            dst[0, p * mz:(p + 1) * mz, :] = high
-            dst[1, p * mz:(p + 1) * mz, :] = low
+            left, right = div[:, :ny // 2], flip(div[:, ny // 2:])
+            for cols, value in ((slice(0, ny // 2), left + right), (slice(ny // 2, ny), left - right)):
+                high, rest = split(value)
+                dst[0, p * mz:(p + 1) * mz, cols] = high
+                dst[1, p * mz:(p + 1) * mz, cols] = rest
 
     def along_y(src, dst):
-        lhs = jnp.concatenate([src[0], src[1], src[0]], axis=1)
-        dst[...] = dot(lhs, jnp.concatenate([sh[...], sh[...], sl[...]], axis=0))
+        fold_dot(src, (eh, el, oh, ol), dst)
 
     def along_z(src):
         for p in range(planes):
@@ -219,23 +272,23 @@
         t_e, t_o = jnp.sum(hits[0], axis=1), jnp.sum(hits[1], axis=1)
         pay[2 * mz:2 * mz + n, :] = pay[2 * mz:2 * mz + n, :] - (t_o + t_e)
         pay[2 * mz + n:2 * mz + 2 * n, :] = t_o - t_e
-        pay_t[...] = pack(pay, mz, n)[:, 0:pay_t.shape[1]]
-
-
-def front(u, v, w, u_lo, u_hi, w_lo, w_hi):
+        pay_t[...] = pack(pay, low, mz, n, mc)[:, 0:pay_t.shape[1]]
+
+
+def front(u, v, w, u_lo, u_hi, w_lo, w_hi, owners):
     n, mz, ny = u.shape
     planes = 2
     steps = n // planes
-    r, edge = mode_planes(mz, ny)
+    r, edge = mode_planes(mz, ny, owners)
     whole = lambda a: pl.BlockSpec(a.shape, lambda i: (0,) * a.ndim, pipeline_mode=pl.Buffered(1))
     here = lambda i: jnp.minimum(i, steps - 1)
     group = pl.BlockSpec((planes, mz, ny), lambda i: (here(i), 0, 0))
-    tables = split_np(0.5 * sine_table(ny)) + split_np(slab_table(mz)) + (r, edge)
+    tables = folded_tables(ny, owners, 0.5) + split_np(slab_table(mz)) + (r, edge)
     prev = pl.BlockSpec((1, mz, ny), lambda i: (jnp.maximum(here(i) * planes - 1, 0), 0, 0))
     after = pl.BlockSpec((1, mz, ny), lambda i: (jnp.minimum(i * planes + planes, n - 1), 0, 0))
     rows = width_of(mz, n)
     return pl.pallas_call(
-        functools.partial(front_kernel, planes, steps),
+        functools.partial(front_kernel, planes, steps, ny // owners),
         grid=(steps + 2,),
         in_specs=[whole(u_lo), whole(u_hi), prev, group, after, group, group, whole(w_lo), whole(w_hi)] + [whole(t) for t in tables],
         out_specs=[pl.BlockSpec((planes, mz, ny), lambda i: (jnp.maximum(i - 2, 0), 0, 0)),
@@ -245,19 +298,19 @@
                         pltpu.VMEM((2, planes * mz, ny), jnp.bfloat16), pltpu.VMEM((2, planes * mz, ny), jnp.bfloat16),
                         pltpu.VMEM((planes * mz, ny), jnp.float32), pltpu.VMEM((planes * mz, ny), jnp.float32),
                         pltpu.VMEM((2, n, 8, ny), jnp.float32), pltpu.VMEM((round_up(rows), ny), jnp.float32),
-                        pltpu.VMEM((2, n, ny), jnp.float32)],
+                        pltpu.VMEM((3 * piece_of(mz, n), ny), jnp.float32), pltpu.VMEM((2, n, ny), jnp.float32)],
         compiler_params=pltpu.CompilerParams(dimension_semantics=("arbitrary",), vmem_limit_bytes=VMEM_LIMIT),
         name="front",
     )(u_lo, u_hi, u, u, u, v, w, w_lo, w_hi, *tables)
 
 
 def owner_kernel(ngx, ngz, n, recv, r, rn, wrap, gain, edge, first, last, inv, xh, xl, jh, jl,
-                 out, buf, hits, mixed, res):
+                 out, buf, hits, mixed, res, low):
     mz, lanes = r.shape
     half = mz // 2
     mc = lanes // (ngx * ngz)
     step = ngz * mc
-    unpack(buf, recv, mz, n)
+    unpack(buf, low, recv, mz, n, mc)
     hits[...] = jnp.zeros_like(hits)
 
     def carries(up, down, rows):
@@ -297,8 +350,8 @@
             hits[1, side, n - 1 - k] = hits[1, side, n - 1 - k] + fold(value)
             return rr * value
 
-        lax.fori_loop(0, n, rise, res[rows, :], unroll=4)
-        lax.fori_loop(0, n, fall, res[below(rows), :], unroll=4)
+        lax.fori_loop(0, n, rise, res[rows, :], unroll=True)
+        lax.fori_loop(0, n, fall, res[below(rows), :], unroll=True)
 
     def beside(field, before):
         if ngz == 1:
@@ -328,9 +381,9 @@
         rr = r[rows, :]
         side = 0 if rows.start < half else 1
         zero = jnp.zeros_like(rr)
-        up = lax.fori_loop(0, n, lambda x, t: rr * t + mixed[side, pl.ds(x, 1), :], zero, unroll=4)
+        up = lax.fori_loop(0, n, lambda x, t: rr * t + mixed[side, pl.ds(x, 1), :], zero, unroll=True)
         buf[rows, :] = buf[rows, :] - edge[rows, :] * up
-        down = lax.fori_loop(0, n, lambda k, t: rr * (t + mixed[side, pl.ds(n - 1 - k, 1), :]), zero, unroll=4)
+        down = lax.fori_loop(0, n, lambda k, t: rr * (t + mixed[side, pl.ds(n - 1 - k, 1), :]), zero, unroll=True)
         buf[below(rows), :] = buf[below(rows), :] - edge[rows, :] * down
     for rows in chunks(mz, 16):
         up, down = carries(buf[rows, :], buf[below(rows), :], rows)
@@ -338,7 +391,7 @@
         res[below(rows), :] = down
     res[0:1, :] = pltpu.roll(g[n - 1:n], step, 1)
     res[mz:mz + 1, :] = pltpu.roll(g[0:1], lanes - step, 1)
-    out[...] = pack(res, mz, n)[:, 0:out.shape[1]]
+    out[...] = pack(res, low, mz, n, mc)[:, 0:out.shape[1]]
 
 
 def owner_tables(ngx, ngz, n, mz, ny):
@@ -346,7 +399,7 @@
     mc = ny // ndev
     start = (lax.axis_index("gx") * ngz + lax.axis_index("gz")) * mc
     order = slab_order(mz)
-    wall = lax.dynamic_slice_in_dim(jnp.asarray(wall_part(ny), jnp.float32), start, mc)
+    wall = lax.dynamic_slice_in_dim(jnp.asarray(wall_part(ny, ndev), jnp.float32), start, mc)
     across = jnp.asarray(np.sin(np.pi * order / (2 * mz)) ** 2, jnp.float32)[:, None]
     real = jnp.asarray(order > 0, jnp.float32)[:, None]
     s = jnp.sqrt(wall + across)
@@ -367,7 +420,7 @@
     slab = np.arange(ny) // mc % ngz
     first = jnp.asarray((slab == 0)[None], jnp.float32)
     last = jnp.asarray((slab == ngz - 1)[None], jnp.float32)
-    edge = mode_planes(mz, ny)[1]
+    edge = mode_planes(mz, ny, ndev)[1]
     sides = split_np(hartley_table(nx)) + split_np(np.kron(hartley_table(ngz), np.eye(mc)))
     return (r, rn, wrap, gain, edge, first, last, jnp.concatenate(inv, axis=1)) + sides
 
@@ -378,14 +431,15 @@
         functools.partial(owner_kernel, ngx, ngz, n),
         out_shape=jax.ShapeDtypeStruct((ny, width), jnp.bfloat16),
         scratch_shapes=[pltpu.VMEM((round_up(width), ny), jnp.float32), pltpu.VMEM((2, 2, n, 8, ny), jnp.float32),
-                        pltpu.VMEM((2, n, ny), jnp.float32), pltpu.VMEM((round_up(width), ny), jnp.float32)],
+                        pltpu.VMEM((2, n, ny), jnp.float32), pltpu.VMEM((round_up(width), ny), jnp.float32),
+                        pltpu.VMEM((3 * piece_of(mz, n), ny), jnp.float32)],
         compiler_params=pltpu.CompilerParams(vmem_limit_bytes=VMEM_LIMIT),
         name="owner",
     )(recv, *tables)
 
 
-def back_kernel(n, a_hbm, ret, u, v, w, sh, sl, th, tl, r, edge, stiff,
-                p_out, u_out, v_out, w_out, a_all, now, xa, xb, pa, pb, rt, rims, sems):
+def back_kernel(n, mc, a_hbm, ret, u, v, w, eh, el, oh, ol, th, tl, r, edge, stiff,
+                p_out, u_out, v_out, w_out, a_all, now, xa, xb, pa, pb, rt, low, rims, modes, sems):
     s = pl.program_id(0)
     mz, ny = now.shape
     half = mz // 2
@@ -399,7 +453,7 @@
         copies = [pltpu.make_async_copy(a_hbm.at[x], a_all.at[x + 1], sems.at[x]) for x in range(n)]
         for copy in copies:
             copy.start()
-        unpack(rt, ret, mz, n)
+        unpack(rt, low, ret, mz, n, mc)
         rims[...] = jnp.zeros_like(rims)
         rims[1:2, :] = rt[0:1, :]
         rims[2:2 + n, :] = rt[2 * mz:2 * mz + n, :]
@@ -433,23 +487,25 @@
             now[0:1, :] = jnp.zeros((1, ny), jnp.float32)
             left = jnp.concatenate([th[...], th[...], tl[...]], axis=1)
             pz = dot(left, jnp.concatenate([hat[0], hat[1], hat[0]], axis=0))
-            high, low = split(pz)
+            high, rest = split(pz)
             base = t * tall
             dst[0, base:base + mz, :] = high
-            dst[1, base:base + mz, :] = low
+            dst[1, base:base + mz, :] = rest
             under = (a_all[jnp.minimum(x + 1, n), 0:1, :] - pz[1:2, :] - line(x + 1) - line(x - 1)
                      + stiff[...] * line(x))
             at = lax.broadcasted_iota(jnp.int32, (EXTRA, ny), 0)
             extra = jnp.where(at == 0, line_next(x), jnp.where(at == EXTRA - 1, under, 0.0))
-            high, low = split(extra)
+            high, rest = split(extra)
             dst[0, base + mz:base + tall, :] = high
-            dst[1, base + mz:base + tall, :] = low
+            dst[1, base + mz:base + tall, :] = rest
 
     def along_y(src, dst):
-        lhs = jnp.concatenate([src[0], src[1], src[0]], axis=1)
-        fresh = dot(lhs, jnp.concatenate([sh[...], sh[...], sl[...]], axis=0))
+        fold_dot(src, (eh, el, oh, ol), modes)
         for t in range(2):
-            dst[t] = fresh[t * tall:(t + 1) * tall]
+            rows = slice(t * tall, (t + 1) * tall)
+            even, odd = modes[rows, :ny // 2], modes[rows, ny // 2:]
+            dst[t, :, :ny // 2] = even + odd
+            dst[t, :, ny // 2:] = flip(even - odd)
 
     def finish(old, new):
         trio = ((1, old[0, :mz], old[1], new[0, :mz]), (0, old[1, :mz], new[0], new[1, :mz]))
@@ -486,17 +542,17 @@
         finish(ps[1 - last % 2], ps[last % 2])
 
 
-def back(a_loc, ret, u, v, w):
+def back(a_loc, ret, u, v, w, owners):
     n, mz, ny = u.shape
-    r, edge = mode_planes(mz, ny)
-    stiff = jnp.asarray(4.0 + 4.0 * wall_part(ny)[None], jnp.float32)
-    tables = split_np(sine_table(ny)) + split_np(slab_table(mz).T) + (r, edge, stiff)
+    r, edge = mode_planes(mz, ny, owners)
+    stiff = jnp.asarray(4.0 + 4.0 * wall_part(ny, owners)[None], jnp.float32)
+    tables = tuple(t.T for t in folded_tables(ny, owners, 1.0)) + split_np(slab_table(mz).T) + (r, edge, stiff)
     whole = lambda a: pl.BlockSpec(a.shape, lambda i: (0,) * a.ndim, pipeline_mode=pl.Buffered(1))
     pair = pl.BlockSpec((2, mz, ny), lambda s: (jnp.clip(n // 2 + 1 - s, 0, n // 2 - 1), 0, 0))
     shape = jax.ShapeDtypeStruct((n, mz, ny), jnp.float32)
     tall = mz + EXTRA
     return pl.pallas_call(
-        functools.partial(back_kernel, n),
+        functools.partial(back_kernel, n, ny // owners),
         grid=(n // 2 + 2,),
         in_specs=[pl.BlockSpec(memory_space=pl.ANY), whole(ret)] + [pair] * 3 + [whole(t) for t in tables],
         out_specs=[pair] * 4,
@@ -504,8 +560,9 @@
         scratch_shapes=[pltpu.VMEM((n + 1, mz, ny), jnp.float32), pltpu.VMEM((mz, ny), jnp.float32),
                         pltpu.VMEM((2, 2 * tall, ny), jnp.bfloat16), pltpu.VMEM((2, 2 * tall, ny), jnp.bfloat16),
                         pltpu.VMEM((2, tall, ny), jnp.float32), pltpu.VMEM((2, tall, ny), jnp.float32),
-                        pltpu.VMEM((round_up(ret.shape[1]), ny), jnp.float32), pltpu.VMEM((n + 8, ny), jnp.float32),
-                        pltpu.SemaphoreType.DMA((n,))],
+                        pltpu.VMEM((round_up(ret.shape[1]), ny), jnp.float32),
+                        pltpu.VMEM((3 * piece_of(mz, n), ny), jnp.float32), pltpu.VMEM((n + 8, ny), jnp.float32),
+                        pltpu.VMEM((2 * tall, ny), jnp.float32), pltpu.SemaphoreType.DMA((n,))],
         compiler_params=pltpu.CompilerParams(dimension_semantics=("arbitrary",), vmem_limit_bytes=VMEM_LIMIT),
         name="back",
     )(a_loc, ret, u, v, w, *tables)
@@ -518,14 +575,14 @@
     tables = owner_tables(ngx, ngz, n, mz, ny)
     w_lo, w_hi = shift_pair(w[:, 0], w[:, -1], "gz")
     u_lo, u_hi = shift_pair(u[:1], u[-1:], "gx")
-    a_loc, pay = front(u, v, w, u_lo, u_hi, w_lo, w_hi)
+    a_loc, pay = front(u, v, w, u_lo, u_hi, w_lo, w_hi, ndev)
 
     def swap(message):
         parts = message.reshape(ndev, ny // ndev, -1)
         return lax.all_to_all(parts, ("gx", "gz"), 0, 0).reshape(ny, -1)
 
     ret = swap(owner(swap(pay), tables, ngx, ngz, n, mz))
-    return back(a_loc, ret, u, v, w)
+    return back(a_loc, ret, u, v, w, ndev)
 
 
 def solution(mesh):

time: 205 us -> 181 us (0.88)
  Pallas kernels: 130 us -> 115 us
  blocking collectives: 28.5 us -> 24.4 us
  waiting for transfers between devices: 22.2 us -> 18.3 us
    pallas_call x2, Pallas kernels: 110 us -> 99.7 us  [the longest x1 52.7 us: back(): pl.pallas_call(functools.partial(back_kernel, n, ny // owners), grid=(n /...]
    pallas_call x1, Pallas kernels: 20.6 us -> 15 us  [owner(): pl.pallas_call(functools.partial(owner_kernel, ngx, ngz, n), out_shape=ja...]
    all_to_all x1, blocking collectives: 28.5 us -> 24.4 us  [swap(): return lax.all_to_all(parts, ('gx', 'gz'), 0, 0).reshape(ny, -1)]
    all_to_all x1, waiting for transfers between devices: 18.4 us -> 14.4 us  [swap(): return lax.all_to_all(parts, ('gx', 'gz'), 0, 0).reshape(ny, -1)]
where the time goes in v3:
time: 181 us; the launch traced here: 180 us
  Pallas kernels  115 us (64%)
  blocking collectives  24.4 us (13%)
  waiting for transfers between devices  18.3 us (10%)
  starting transfers between devices  11.6 us (6%)
  local copies, waits for them, and re-layouts  10.1 us (6%)
    pallas_call x1, Pallas kernels, back(): pl.pallas_call(functools.partial(back_kernel, n, ny // owners), grid=(n /...  52.7 us
    pallas_call x1, Pallas kernels, front(): pl.pallas_call(functools.partial(front_kernel, planes, steps, ny // owner...  47 us
    all_to_all x1, blocking collectives, swap(): return lax.all_to_all(parts, ('gx', 'gz'), 0, 0).reshape(ny, -1)  24.4 us
    pallas_call x1, Pallas kernels, owner(): pl.pallas_call(functools.partial(owner_kernel, ngx, ngz, n), out_shape=ja...  15 us
    all_to_all x1, waiting for transfers between devices, swap(): return lax.all_to_all(parts, ('gx', 'gz'), 0, 0).reshape(ny, -1)  14.4 us
    all_to_all x1, starting transfers between devices, swap(): return lax.all_to_all(parts, ('gx', 'gz'), 0, 0).reshape(ny, -1)  7.33 us
    another operation x8, local copies, waits for them, and re-layouts, owner_tables(): wide = lambda t: jnp.tile(t * real, (1, ndev))  4.47 us
    ppermute x2, starting transfers between devices, shift_pair(): lax.ppermute(last, axis, forward)  3.91 us
  transfers between devices with their start and end apart: 5, of which 4 were waited for; matrix products, arithmetic and copies ran while one was open for 4% of the time, Pallas kernels for 0%

profile of v3, /device:TPU:1, one launch (start us, length us, event | category | flops | bytes accessed | tf_op | source)
XLA Modules:
  0.0 180.4 jit_solution(7654292268105816886)
XLA Ops:
  0.6 1.1 fusion.14
  1.7 0.1 collective-permute-start.1
  1.8 2.6 %collective-permute-start = (bf16[1,192,768]{2,1,0:T(8,128)(2,1)S(1)}, bf16[1,192,768]{2,1,0:T(8,128)(2,1)S(1)}, u32[]{:S(2)}, u32[]{:S(2)}) collective-permute-start(bf16[1,192,768]{2,1,0:T(8,128)(2,1)S(1)} %get-tuple-element.11), channel_id=1, source_target_pairs={{0,2},{2,4},{4,6},{6,8},{8,10},{10,12},{12,14},{14,16},{16,18},{18... | collective-permute-start | bytes 884744 | tf_op jit(solution)/shard_map/ppermute | solution.py:61
  4.4 1.3 fusion.13
  5.7 1.3 collective-permute-start.2
  7.1 0.0 copy-start.5
  7.1 0.0 copy-start.6
  7.1 0.0 copy-start.8
  7.1 0.3 collective-permute-start.3
  7.4 1.3 collective-permute-done.2.w_lo
  8.7 1.4 collective-permute-done.3.w_hi
  10.1 1.2 collective-permute-done.u_lo
  11.3 0.7 copy-done.2
  12.0 47.0 %front.1 = (f32[32,192,768]{2,1,0:T(8,128)}, bf16[768,512]{1,0:T(8,128)(2,1)}) custom-call(bf16[1,192,768]{2,1,0:T(8,128)(2,1)} %copy-done.2, bf16[1,192,768]{2,1,0:T(8,128)(2,1)} %copy-done.1, bf16[32,192,768]{2,1,0:T(8,128)(2,1)} %u.3, bf16[32,192,768]{2,1,0:T(8,128)(2,1)} %u.3, bf16[32,192,768]{2,1,0:T(8,128)(2,1)} %u.3, bf16[32,192,768]{2,1,0:T(8,128)(2,1)} %v.3, ...), custom_call_target="tpu_custom_call" | custom-call | tf_op jit(solution)/shard_map/front/pallas_call | solution.py:290
  59.0 7.3 %all-to-all-start = ((bf16[32,24,512]{2,1,0:T(8,128)(2,1)}), bf16[32,24,512]{2,1,0:T(8,128)(2,1)S(1)}, u32[]{:S(2)}, u32[]{:S(2)}) async-start(bf16[32,24,512]{2,1,0:T(8,128)(2,1)} %bitcast.21), calls=%async_computation | async-start | bytes 1572864 | tf_op jit(solution)/shard_map/all_to_all | solution.py:582
  66.3 0.8 dynamic_slice.3
  67.1 0.2 fusion.10
  67.3 0.9 copy.50.inv
  68.2 0.1 divide_multiply_fusion
  68.3 0.1 tile.42
  68.4 1.1 copy.49.gain
  69.4 0.1 tile.18
  69.5 1.1 copy.47.rn
  70.5 0.1 tile.40
  70.6 1.1 copy.48.wrap
  71.7 0.1 tile.16
  71.7 1.1 copy.46.r
  72.8 14.4 %all-to-all-done = bf16[32,24,512]{2,1,0:T(8,128)(2,1)S(1)} async-done(((bf16[32,24,512]{2,1,0:T(8,128)(2,1)}), bf16[32,24,512]{2,1,0:T(8,128)(2,1)S(1)}, u32[]{:S(2)}, u32[]{:S(2)}) %all-to-all-start) | async-done | bytes 786464 | tf_op jit(solution)/shard_map/all_to_all | solution.py:582
  87.2 0.9 copy-done
  88.1 15.0 %owner.1 = bf16[768,512]{1,0:T(8,128)(2,1)} custom-call(bf16[768,512]{1,0:T(8,128)(2,1)} %bitcast.14, f32[192,768]{1,0:T(8,128)} %copy.46.r, f32[192,768]{1,0:T(8,128)} %copy.47.rn, f32[192,768]{1,0:T(8,128)} %copy.48.wrap, f32[192,768]{1,0:T(8,128)} %copy.49.gain, f32[192,768]{1,0:T(8,128)} %constant.93.clone.edge, f32[1,768]{1,0:T(1,128)} %constant.91.clone.first, ...), custom_call_target="tpu_custom_call" | custom-call | tf_op jit(solution)/shard_map/owner/pallas_call | solution.py:430
  103.2 24.4 %all_to_all.10 = bf16[32,24,512]{2,1,0:T(8,128)(2,1)} all-to-all(bf16[32,24,512]{2,1,0:T(8,128)(2,1)} %bitcast.15), channel_id=1, replica_groups=mesh['gx'=16,'gz'=2] {'gx','gz'}, dimensions={0} | all-to-all | bytes 1572864 | tf_op jit(solution)/shard_map/all_to_all | solution.py:582
  127.5 52.7 %back.1 = (f32[32,192,768]{2,1,0:T(8,128)}, f32[32,192,768]{2,1,0:T(8,128)}, f32[32,192,768]{2,1,0:T(8,128)}, f32[32,192,768]{2,1,0:T(8,128)}) custom-call(f32[32,192,768]{2,1,0:T(8,128)} %get-tuple-element.6.a_hbm, bf16[768,512]{1,0:T(8,128)(2,1)} %bitcast.20, bf16[32,192,768]{2,1,0:T(8,128)(2,1)} %u.3, bf16[32,192,768]{2,1,0:T(8,128)(2,1)} %v.3, ...), custom_call_target="tpu_custom_call" | custom-call | tf_op jit(solution)/shard_map/back/pallas_call | solution.py:554
  (17 shorter events, 0.1 us)
Async XLA Ops:
  1.7 8.4 %collective-permute-start.1 = (bf16[1,192,768]{2,1,0:T(8,128)(2,1)S(1)}, bf16[1,192,768]{2,1,0:T(8,128)(2,1)S(1)}, u32[]{:S(2)}, u32[]{:S(2)}) collective-permute-start(bf16[1,192,768]{2,1,0:T(8,128)(2,1)S(1)} %get-tuple-element.10), channel_id=1, source_target_pairs={{2,0},{4,2},{6,4},{8,6},{10,8},{12,10},{14,12},{16,14},{18,16},{20... | collective-permute-start | bytes 884744 | tf_op jit(solution)/shard_map/ppermute | solution.py:61
  1.8 9.4 %collective-permute-start = (bf16[1,192,768]{2,1,0:T(8,128)(2,1)S(1)}, bf16[1,192,768]{2,1,0:T(8,128)(2,1)S(1)}, u32[]{:S(2)}, u32[]{:S(2)}) collective-permute-start(bf16[1,192,768]{2,1,0:T(8,128)(2,1)S(1)} %get-tuple-element.11), channel_id=1, source_target_pairs={{0,2},{2,4},{4,6},{6,8},{8,10},{10,12},{12,14},{14,16},{16,18},{18... | collective-permute-start | bytes 884744 | tf_op jit(solution)/shard_map/ppermute | solution.py:61
  5.7 3.0 %collective-permute-start.2 = (bf16[32,768]{1,0:T(8,128)(2,1)S(1)}, bf16[32,768]{1,0:T(8,128)(2,1)S(1)}, u32[]{:S(2)}, u32[]{:S(2)}) collective-permute-start(bf16[32,768]{1,0:T(8,128)(2,1)S(1)} %bitcast.22), channel_id=1, source_target_pairs={{0,1},{1,0},{2,3},{3,2},{4,5},{5,4},{6,7},{7,6},{8,9},{9,8},{10,11... | collective-permute-start | bytes 147464 | tf_op jit(solution)/shard_map/ppermute | solution.py:61
  7.1 60.0 %copy-start.5 = (f32[512]{0:T(512)S(1)}, f32[512]{0:T(512)}, u32[]{:S(2)}) copy-start(f32[512]{0:T(512)} %constant.90.clone) | copy-start | bytes 6148
  7.1 61.1 %copy-start.6 = (f32[192]{0:T(256)S(1)}, f32[192]{0:T(256)}, u32[]{:S(2)}) copy-start(f32[192]{0:T(256)} %constant.113) | copy-start | bytes 2308
  7.1 61.1 %copy-start.7 = (f32[192]{0:T(256)S(1)}, f32[192]{0:T(256)}, u32[]{:S(2)}) copy-start(f32[192]{0:T(256)} %constant.88.clone) | copy-start | bytes 2308
  7.1 61.1 %copy-start.8 = (f32[192]{0:T(256)S(1)}, f32[192]{0:T(256)}, u32[]{:S(2)}) copy-start(f32[192]{0:T(256)} %constant.87.clone) | copy-start | bytes 2308
  7.1 3.0 %collective-permute-start.3 = (bf16[32,768]{1,0:T(8,128)(2,1)S(1)}, bf16[32,768]{1,0:T(8,128)(2,1)S(1)}, u32[]{:S(2)}, u32[]{:S(2)}) collective-permute-start(bf16[32,768]{1,0:T(8,128)(2,1)S(1)} %bitcast.23), channel_id=1, source_target_pairs={{1,0},{0,1},{3,2},{2,3},{5,4},{4,5},{7,6},{6,7},{9,8},{8,9},{11,10... | collective-permute-start | bytes 147464 | tf_op jit(solution)/shard_map/ppermute | solution.py:61
  8.7 2.5 %copy-start.3 = (bf16[32,768]{1,0:T(8,128)(2,1)}, bf16[32,768]{1,0:T(8,128)(2,1)S(1)}, u32[]{:S(2)}) copy-start(bf16[32,768]{1,0:T(8,128)(2,1)S(1)} %collective-permute-done.2.w_lo) | copy-start | bytes 147460
  10.1 1.2 copy-start.4
  10.1 1.2 copy-start.1
  11.3 0.7 copy-start.2
  59.0 28.2 %all-to-all-start = ((bf16[32,24,512]{2,1,0:T(8,128)(2,1)}), bf16[32,24,512]{2,1,0:T(8,128)(2,1)S(1)}, u32[]{:S(2)}, u32[]{:S(2)}) async-start(bf16[32,24,512]{2,1,0:T(8,128)(2,1)} %bitcast.21), calls=%async_computation | async-start | bytes 1572864 | tf_op jit(solution)/shard_map/all_to_all | solution.py:582
  87.2 0.9 copy-start
